TPU v7x, 1024 devices: a whole 4x4x32 slice. The times are simulated.
1024 devices in a mesh: row: 64 (over z_lo, y), col: 16 (over x, z_hi, core).
Axes of the slice: x: 4, y: 4, z: 32 (z_hi: 2, z_lo: 16; z = z_hi * 16 + z_lo), core: 2. Of those that a mesh axis runs over, the one named last changes fastest.
Arguments:
- features: bfloat16 [131072, 256], P('row', 'col'), may hold values from -6 to 6
- tile_values: bfloat16 [64, 192, 128, 128], P('row'), may hold values from -0.15625 to 0.15625
- tile_rows: int32 [64, 192], replicated, may hold values from 0 to 15
- tile_cols: int32 [64, 192], replicated, may hold values from 0 to 1023, as said below
- tile_count: int32 [64], replicated, may hold values from 32 to 192, as said below
- weight: bfloat16 [256, 256], replicated, may hold values from -0.375 to 0.375
- out_bias: float32 [256], replicated, may hold values from -3 to 3
- cotangent: bfloat16 [131072, 256], P('row', 'col'), may hold values from -6 to 6
Outputs:
- activated: bfloat16 [131072, 256], P('row', 'col')
- feature_grad: bfloat16 [131072, 256], P('row', 'col')
- weight_grad: float32 [256, 256], P('col')
- bias_grad: float32 [256], P('col')
Inputs may be any that keep to these rules, and one draw needn't show every extreme that they name: tile_cols[g, s] names a tile column of row group g - 1, g or g + 1, counted cyclically over the 64 row groups, where row group h holds tile columns h * 16 to h * 16 + 15. `tile_count`: the live slots of a row group are its first ones; exactly one row group fills all 192 slots in every draw, and every other one has at most 64 live slots.
All inputs are finite; a program needn't handle non-finite values.
Results may differ from a plain program's by a relative error of at most 0.007.
Values may be sent and summed in bfloat16 or wider, within the bound.
A program may use at most 64 MiB of HBM per device.

v0:
```python
import math

import jax
import jax.numpy as jnp
from jax import lax
from jax.sharding import PartitionSpec as P

GROUP_SLOTS = 16


def with_halo(x, sides, width):
    for axis, dim in sides:
        size, length = (lax.axis_size(axis), x.shape[dim])
        up = [(i, (i + 1) % size) for i in range(size)]
        down = [(j, i) for i, j in up]
        last = lax.slice_in_dim(x, length - width, length, axis=dim)
        initial = lax.slice_in_dim(x, 0, width, axis=dim)
        before = lax.ppermute(last, axis, up)
        after = lax.ppermute(initial, axis, down)
        x = jnp.concatenate([before, x, after], axis=dim)
    return x


def passed_along(value, axis, steps):
    count = lax.axis_size(axis)
    pairs = [(source, (source + steps) % count) for source in range(count)]
    return lax.ppermute(value, axis, pairs)


def relative_columns(columns, owner, row_tiles, row_total):
    return (
        columns // row_tiles - owner + 1 + row_total
    ) % row_total * row_tiles + columns % row_tiles


def select_slots(arrays, stride, offset):
    amount = arrays[0].shape[0] // stride
    picked = []
    for source in arrays:
        shaped = source.reshape((amount, stride) + source.shape[1:])
        picked.append(lax.dynamic_index_in_dim(shaped, offset, 1, keepdims=False))
    return tuple(picked)


def tile_products(slot_set, live_count, window, row_tiles):
    values, slot_rows, rel_cols, slot_ids = slot_set
    tile_size = values.shape[-1]
    feat_width = window.shape[-1]
    blocks = window.reshape(-1, tile_size, feat_width)
    step_slots = math.gcd(GROUP_SLOTS, values.shape[0])
    targets = jnp.arange(row_tiles, dtype=jnp.int32)

    def advance(turn_index, running):
        slot_start = turn_index * step_slots
        part_values = lax.dynamic_slice_in_dim(values, slot_start, step_slots, 0)
        part_rows = lax.dynamic_slice_in_dim(slot_rows, slot_start, step_slots, 0)
        part_cols = lax.dynamic_slice_in_dim(rel_cols, slot_start, step_slots, 0)
        part_ids = lax.dynamic_slice_in_dim(slot_ids, slot_start, step_slots, 0)
        live_slots = part_ids < live_count
        gathered = jnp.take(blocks, part_cols, axis=0)
        product = jnp.einsum(
            "sij,sjf->sif", part_values, gathered, preferred_element_type=jnp.float32
        )
        selector = ((part_rows[:, None] == targets[None, :]) & live_slots[:, None]).astype(
            jnp.float32
        )
        return running + jnp.einsum(
            "st,sif->tif", selector, product, precision=lax.Precision.HIGHEST
        )

    live_total = jnp.sum((slot_ids < live_count).astype(jnp.int32))
    turn_total = (live_total + step_slots - 1) // step_slots
    running = lax.fori_loop(
        0, turn_total, advance, jnp.zeros((row_tiles, tile_size, feat_width), jnp.float32)
    )
    return running.reshape(row_tiles * tile_size, feat_width)


def tile_transposed(slot_set, live_count, inner_grad, row_tiles):
    values, slot_rows, rel_cols, slot_ids = slot_set
    tile_size = values.shape[-1]
    feat_width = inner_grad.shape[-1]
    blocks = inner_grad.reshape(row_tiles, tile_size, feat_width)
    step_slots = math.gcd(GROUP_SLOTS, values.shape[0])
    targets = jnp.arange(3 * row_tiles, dtype=jnp.int32)

    def advance(turn_index, running):
        slot_start = turn_index * step_slots
        part_values = lax.dynamic_slice_in_dim(values, slot_start, step_slots, 0)
        part_rows = lax.dynamic_slice_in_dim(slot_rows, slot_start, step_slots, 0)
        part_cols = lax.dynamic_slice_in_dim(rel_cols, slot_start, step_slots, 0)
        part_ids = lax.dynamic_slice_in_dim(slot_ids, slot_start, step_slots, 0)
        live_slots = part_ids < live_count
        gathered = jnp.take(blocks, part_rows, axis=0)
        product = jnp.einsum(
            "sij,sif->sjf", part_values, gathered, preferred_element_type=jnp.float32
        )
        selector = ((part_cols[:, None] == targets[None, :]) & live_slots[:, None]).astype(
            jnp.float32
        )
        return running + jnp.einsum(
            "sw,sjf->wjf", selector, product, precision=lax.Precision.HIGHEST
        )

    live_total = jnp.sum((slot_ids < live_count).astype(jnp.int32))
    turn_total = (live_total + step_slots - 1) // step_slots
    running = lax.fori_loop(
        0, turn_total, advance, jnp.zeros((3 * row_tiles, tile_size, feat_width), jnp.float32)
    )
    return running.reshape(3, row_tiles * tile_size, feat_width)


def on_device(features, tile_values, tile_rows, tile_cols, tile_count, weight, out_bias, cotangent):
    tile_size = tile_values.shape[-1]
    node_rows = features.shape[0]
    row_tiles = node_rows // tile_size
    slice_width = features.shape[1]
    slot_total = tile_values.shape[1]
    row_total = lax.axis_size("row")
    row_index = lax.axis_index("row")
    col_index = lax.axis_index("col")
    values = tile_values[0]
    slot_ids = jnp.arange(slot_total, dtype=jnp.int32)
    own_rows = lax.dynamic_index_in_dim(tile_rows, row_index, 0, keepdims=False)
    own_cols = relative_columns(
        lax.dynamic_index_in_dim(tile_cols, row_index, 0, keepdims=False),
        row_index,
        row_tiles,
        row_total,
    )
    own_count = lax.dynamic_index_in_dim(tile_count, row_index, 0, keepdims=False)
    col_start = col_index * slice_width
    stride = 1
    offset = 0
    own_full = (values, own_rows, own_cols, slot_ids)
    full_rows = lax.all_gather(features, "col", axis=1, tiled=True)
    window = with_halo(full_rows, (("row", 0),), node_rows)
    own_part = tile_products(select_slots(own_full, stride, offset), own_count, window, row_tiles)
    stacked = own_part[None]
    own_sum = stacked[0]
    hidden_full = own_sum.astype(jnp.bfloat16)
    hidden_own = lax.dynamic_slice_in_dim(hidden_full, col_start, slice_width, 1)
    weight_cols = lax.dynamic_slice_in_dim(weight, col_start, slice_width, 1)
    bias_own = lax.dynamic_slice_in_dim(out_bias, col_start, slice_width, 0)
    preact = jnp.dot(hidden_full, weight_cols, preferred_element_type=jnp.float32) + bias_own
    sigma = jax.nn.sigmoid(preact)
    activated = (preact * sigma).astype(jnp.bfloat16)
    grad_own = (cotangent.astype(jnp.float32) * sigma * (1.0 + preact * (1.0 - sigma))).astype(
        jnp.bfloat16
    )
    grad_full = lax.all_gather(grad_own, "col", axis=1, tiled=True)
    weight_rows = lax.dynamic_slice_in_dim(weight, col_start, slice_width, 0)
    inner_grad = lax.dot_general(
        grad_full, weight_rows, (((1,), (1,)), ((), ())), preferred_element_type=jnp.float32
    ).astype(jnp.bfloat16)
    weight_part = lax.dot_general(
        hidden_own, grad_full, (((0,), (0,)), ((), ())), preferred_element_type=jnp.float32
    )
    bias_part = jnp.sum(grad_own.astype(jnp.float32), axis=0)
    own_spread = tile_transposed(own_full, own_count, inner_grad, row_tiles)
    lower_terms = own_spread[0]
    middle_terms = own_spread[1]
    upper_terms = own_spread[2]
    from_next = passed_along(lower_terms, "row", -1)
    from_prev = passed_along(upper_terms, "row", 1)
    feature_grad = (middle_terms + from_next + from_prev).astype(jnp.bfloat16)
    weight_sum, bias_sum = lax.psum((weight_part, bias_part), "row")
    scale_factor = 1.0 / math.sqrt(node_rows * row_total)
    return (activated, feature_grad, weight_sum * scale_factor, bias_sum * scale_factor)


def solution(mesh):
    in_specs = (
        P("row", "col"),
        P("row", None, None, None),
        P(),
        P(),
        P(),
        P(),
        P(),
        P("row", "col"),
    )
    out_specs = (P("row", "col"), P("row", "col"), P("col", None), P("col"))
    return jax.shard_map(
        on_device, mesh=mesh, in_specs=in_specs, out_specs=out_specs, check_vma=False
    )
```

profile of v0, /device:TPU:2, one launch (start us, length us, event | category | flops | bytes accessed | tf_op | source)
XLA Modules:
  0.0 1182.4 jit_solution(2973994663431302596)
XLA Ops:
  8.0 134.1 %all-gather.3.cloned.1.call-done = bf16[2048,256]{0,1:T(8,128)(2,1)} async-done(((bf16[2048,16]{0,1:T(8,128)(2,1)}), bf16[2048,256]{0,1:T(8,128)(2,1)}) %all-gather.3.cloned.1.call-update) | async-done | bytes 1048592 | tf_op jit(solution)/shard_map/all_gather | solution.py:136
  142.1 3.4 collective-permute-start
  145.5 20.8 %collective-permute-start.1 = (bf16[2048,256]{0,1:T(8,128)(2,1)}, bf16[2048,256]{0,1:T(8,128)(2,1)}, u32[]{:S(2)}, u32[]{:S(2)}) collective-permute-start(bf16[2048,256]{0,1:T(8,128)(2,1)} %all-gather.3.cloned.1.call-done), channel_id=1, source_target_pairs={{16,0},{32,16},{48,32},{64,48},{80,64},{96,80},{112,96},{128,112},... | collective-permute-start | bytes 3145736 | tf_op jit(solution)/shard_map/ppermute | solution.py:19
  171.6 16.2 %collective-permute-done = bf16[2048,256]{0,1:T(8,128)(2,1)S(1)} collective-permute-done((bf16[2048,256]{0,1:T(8,128)(2,1)}, bf16[2048,256]{0,1:T(8,128)(2,1)S(1)}, u32[]{:S(2)}, u32[]{:S(2)}) %collective-permute-start) | collective-permute-done | bytes 1048608 | tf_op jit(solution)/shard_map/ppermute | solution.py:18
  189.1 2.0 pad_maximum_fusion
  191.1 2.8 copy.14
  194.2 23.8 %while.22 = (s32[]{:T(128)}, f32[16,128,256]{2,0,1:T(8,128)S(1)}, s32[]{:T(128)}, s32[192]{0:T(256)S(1)}, s32[192]{0:T(256)S(1)}, /*index=5*/s32[]{:T(128)}, bf1...) while((s32[]{:T(128)}, f32[16,128,256]{2,0,1:T(8,128)S(1)}, ...), condition=%wide.region_2.3_spmd.clone, body=%wide.region_1.2_spmd.clone.sunk | while | flops 235931248 | bytes 12063483 | solution.py:73
  194.9 2.5 gather_fusion
  197.4 1.6 fusion.67
  199.1 3.0 fusion.68
  202.9 2.5 gather_fusion
  205.4 1.6 fusion.67
  207.0 3.0 fusion.68
  210.8 2.5 gather_fusion
  213.3 1.6 fusion.67
  214.9 3.0 fusion.68
  220.4 154.9 %all-gather.5.cloned.1.call-done = bf16[2048,256]{0,1:T(8,128)(2,1)} async-done(((bf16[2048,16]{0,1:T(8,128)(2,1)}), bf16[2048,256]{0,1:T(8,128)(2,1)}) %all-gather.5.cloned.1.call-update) | async-done | bytes 1048592 | tf_op jit(solution)/shard_map/all_gather | solution.py:151
  375.3 1.8 fusion.35
  377.1 755.6 %all-reduce = (f32[16,256]{1,0:T(8,128)S(1)}, f32[16]{0:T(128)S(1)}) all-reduce(f32[16,256]{1,0:T(8,128)S(1)} %fusion.35, f32[16]{0:T(128)S(1)} %get-tuple-element.214), channel_id=1, replica_groups=mesh['row'=64,'col'=16] {'row'}, use_global_device_ids=true, to_apply=%region_5.6 | all-reduce | flops 4112 | bytes 32896 | tf_op jit(solution)/shard_map/psum | solution.py:167
  1133.3 1.5 fusion.34
  1134.9 9.8 while.23
  1144.7 4.9 collective-permute-start.2
  1149.7 1.9 collective-permute-start.3
  1152.1 22.7 %collective-permute-done.3 = f32[2048,16]{0,1:T(8,128)S(1)} collective-permute-done((f32[2048,16]{0,1:T(8,128)S(1)}, f32[2048,16]{0,1:T(8,128)S(1)}, u32[]{:S(2)}, u32[]{:S(2)}) %collective-permute-start.3) | collective-permute-done | bytes 131104 | tf_op jit(solution)/shard_map/ppermute | solution.py:27
  (57 shorter events, 23.4 us)
Async XLA Ops:
  7.2 211.9 %copy-start = (bf16[256,256]{1,0:T(8,128)(2,1)S(1)}, bf16[256,256]{1,0:T(8,128)(2,1)}, u32[]{:S(2)}) copy-start(bf16[256,256]{1,0:T(8,128)(2,1)} %param.17) | copy-start | bytes 393220
  7.2 134.9 %all-gather.3.cloned.1.call-start = ((), (), s32[]{:S(2)}) async-start(), calls=%async_computation | async-start | bytes 1114112 | tf_op jit(solution)/shard_map/all_gather | solution.py:136
  7.9 367.3 %all-gather.5.cloned.1.call-start = ((), (), s32[]{:S(2)}) async-start(), calls=%async_computation.1 | async-start | bytes 1114112 | tf_op jit(solution)/shard_map/all_gather | solution.py:151
  142.1 45.7 %collective-permute-start = (bf16[2048,256]{0,1:T(8,128)(2,1)}, bf16[2048,256]{0,1:T(8,128)(2,1)S(1)}, u32[]{:S(2)}, u32[]{:S(2)}) collective-permute-start(bf16[2048,256]{0,1:T(8,128)(2,1)} %all-gather.3.cloned.1.call-done), channel_id=1, source_target_pairs={{0,16},{16,32},{32,48},{48,64},{64,80},{80,96},{96,112},{112,128},... | collective-permute-start | bytes 3145736 | tf_op jit(solution)/shard_map/ppermute | solution.py:18
  145.5 43.6 %collective-permute-start.1 = (bf16[2048,256]{0,1:T(8,128)(2,1)}, bf16[2048,256]{0,1:T(8,128)(2,1)}, u32[]{:S(2)}, u32[]{:S(2)}) collective-permute-start(bf16[2048,256]{0,1:T(8,128)(2,1)} %all-gather.3.cloned.1.call-done), channel_id=1, source_target_pairs={{16,0},{32,16},{48,32},{64,48},{80,64},{96,80},{112,96},{128,112},... | collective-permute-start | bytes 3145736 | tf_op jit(solution)/shard_map/ppermute | solution.py:19
  187.8 1.0 copy-start.1
  218.0 1.1 copy-start.2
  1144.7 7.4 collective-permute-start.2
  1149.7 25.2 %collective-permute-start.3 = (f32[2048,16]{0,1:T(8,128)S(1)}, f32[2048,16]{0,1:T(8,128)S(1)}, u32[]{:S(2)}, u32[]{:S(2)}) collective-permute-start(f32[2048,16]{0,1:T(8,128)S(1)} %bitcast.54), channel_id=1, source_target_pairs={{0,16},{16,32},{32,48},{48,64},{64,80},{80,96},{96,112},{112,128},... | collective-permute-start | bytes 393224 | tf_op jit(solution)/shard_map/ppermute | solution.py:27
Sparse Core Ops, SparseCore 0:
  12.4 129.6 all-gather.2
  220.5 154.7 all-gather.4
where the time goes:
time: 1180 us
  blocking collectives  756 us (64%)
  waiting for transfers between devices  329 us (28%)
  starting transfers between devices  31.1 us (3%)
  matrix products  23.7 us (2%)
  local copies, waits for them, and re-layouts  18.5 us (2%)
  between operations  14.9 us (1%)
    psum x1, blocking collectives, on_device(): weight_sum, bias_sum = lax.psum((weight_part, bias_part), 'row')  756 us
    all_gather x1, waiting for transfers between devices, on_device(): grad_full = lax.all_gather(grad_own, 'col', axis=1, tiled=True)  155 us
    all_gather x1, waiting for transfers between devices, on_device(): full_rows = lax.all_gather(features, 'col', axis=1, tiled=True)  134 us
  transfers between devices with their start and end apart: 6, of which 5 were waited for; matrix products, arithmetic and copies ran while one was open for 0% of the time, Pallas kernels for 0%

commit v1 on v0

v1 whole, which is shorter than its diff:
```python
import functools
import math

import jax
import jax.numpy as jnp
from jax import lax
from jax.experimental import pallas as pl
from jax.experimental.pallas import tpu as pltpu
from jax.sharding import PartitionSpec as P

MESH = pl.DeviceIdType.MESH
F32 = jnp.float32
BF16 = jnp.bfloat16
T = 128
TR = 16
W = 16
ROWS = 64
COLS = 16
UNROLL = 8
CHUNKS = 4
NT = (((1,), (1,)), ((), ()))
NN = (((1,), (0,)), ((), ()))


def dot(a, b, dims=NN):
    return lax.dot_general(a, b, dims, preferred_element_type=F32)


def select_sum(onehot, prods, targets, out):
    slots = onehot.shape[1]
    for f in range(W):
        v = prods[pl.ds(f, slots, stride=W), :]
        hi = v.astype(BF16)
        lo = (v - hi.astype(F32)).astype(BF16)
        out[pl.ds(f, targets, stride=W), :] = dot(onehot, hi) + dot(onehot, lo)


def kernel(
    slots,
    scale,
    ft,
    ct,
    tv,
    rows_h,
    cols_h,
    count_h,
    w_h,
    bias_h,
    act_o,
    fg_o,
    wg_o,
    bg_o,
    rows_s,
    cols_s,
    count_s,
    rows_v,
    cols_v,
    w,
    bias,
    win,
    cols3,
    tvv,
    prods,
    sums,
    wt,
    cot_buf,
    agg_send,
    agg_buf,
    ag_send,
    ag_buf,
    act_send,
    act_buf,
    halo_send,
    halo_buf,
    s1_send,
    s1_buf,
    r1_send,
    r1_buf,
    r2_send,
    r2_buf,
    r3_send,
    r3_buf,
    y_send,
    y_buf,
    tile_sem,
    own_sem,
    halo_ss,
    halo_rs,
    back_ss,
    back_rs,
    ss,
    rs,
):
    g = lax.axis_index("row")
    me = lax.axis_index("col")
    z_lo, y = g // 4, g % 4
    za, zb = z_lo // 4, z_lo % 4
    x, zh, core = me // 4, (me // 2) % 2, me % 2
    prev, nxt = (g + ROWS - 1) % ROWS, (g + 1) % ROWS

    col_peers = []
    for dz in (1, 0):
        for dx in (2, 1, 3, 0):
            for dc in (0, 1):
                if (dz, dx, dc) != (0, 0, 0):
                    col_peers.append(((x + dx) % 4) * 4 + ((zh + dz) % 2) * 2 + (core + dc) % 2)
    z_peers = []
    for dx in (2, 1, 3, 0):
        for dy in (2, 1, 3, 0):
            for dc in (0, 1):
                if (dx, dy, dc) != (0, 0, 0):
                    px, py, pc = (x + dx) % 4, (y + dy) % 4, (core + dc) % 2
                    part = 2 * (4 * px + 2 * (py // 2) + pc) + py % 2
                    z_peers.append((z_lo * 4 + py, px * 4 + zh * 2 + pc, part))
    my_part = 2 * (4 * x + 2 * (y // 2) + core) + y % 2
    my_rank = x * 8 + y * 2 + core
    b_peers = [((za * 4 + (zb + d) % 4) * 4 + y, me) for d in (1, 2, 3)]
    a_peers = [((((za + d) % 4) * 4 + zb) * 4 + y, me) for d in (1, 2, 3)]
    h_peers = [(g, x * 4 + ((zh + 1) % 2) * 2 + core)]
    y_peers = [(z_lo * 4 + (y + d) % 4, me) for d in (1, 2, 3)]

    step = slots // CHUNKS
    tile_copies = [
        pltpu.make_async_copy(
            tv.at[0, pl.ds(k * step, step)], tvv.at[pl.ds(k * step, step)], tile_sem.at[k]
        )
        for k in range(CHUNKS)
    ]
    own_ft = pltpu.make_async_copy(ft, win.at[1], own_sem.at[0])
    own_ct = pltpu.make_async_copy(
        ct.at[:, pl.ds(pl.multiple_of(me * T, T), T)], cot_buf.at[me], own_sem.at[1]
    )
    index_copies = [
        pltpu.make_async_copy(src, dst, own_sem.at[2 + k])
        for k, (src, dst) in enumerate(
            (
                (cols_h, cols_s),
                (rows_h, rows_v),
                (cols_h, cols_v),
                (count_h, count_s),
                (w_h, w),
                (bias_h, bias),
                (rows_h, rows_s),
            )
        )
    ]
    for copy in index_copies:
        copy.start()
    own_ft.start()
    own_ct.start()
    for copy in tile_copies:
        copy.start()

    barrier = pltpu.get_barrier_semaphore()
    everyone = (
        [(prev, me), (nxt, me)]
        + [(g, c) for c in col_peers]
        + [(r, c) for r, c, _ in z_peers]
        + b_peers
        + a_peers
        + h_peers
        + y_peers
    )
    for peer in everyone:
        pl.semaphore_signal(barrier, inc=1, device_id=peer, device_id_type=MESH)
    pl.semaphore_wait(barrier, len(everyone))

    def send(src, dst, send_sem, recv_sem, peer):
        copy = pltpu.make_async_remote_copy(
            src_ref=src,
            dst_ref=dst,
            send_sem=send_sem,
            recv_sem=recv_sem,
            device_id=peer,
            device_id_type=MESH,
        )
        copy.start()
        return copy

    def await_blocks(buf, count, sem):
        view = buf.at[pl.ds(0, count)]
        pltpu.make_async_copy(view, view, sem).wait()

    to_prev = send(ft, win.at[2], halo_ss.at[0], halo_rs.at[0], (prev, me))
    to_next = send(ft, win.at[0], halo_ss.at[1], halo_rs.at[1], (nxt, me))
    for c in col_peers:
        send(
            ct.at[:, pl.ds(pl.multiple_of(c * T, T), T)],
            cot_buf.at[me],
            ss.at[0],
            rs.at[0],
            (g, c),
        )

    for copy in index_copies:
        copy.wait()
    count = count_s[g]
    live = lax.broadcasted_iota(jnp.int32, (TR, slots), 1) < count
    row_ids = lax.broadcasted_iota(jnp.int32, (TR, slots), 0)
    by_row = jnp.where((rows_v[pl.ds(g, 1), :] == row_ids) & live, 1.0, 0.0).astype(BF16)
    own_cols = cols_v[pl.ds(g, 1), :]
    rel = ((lax.div(own_cols, TR) - g + (ROWS + 1)) % ROWS) * TR + lax.rem(own_cols, TR)
    by_col = [
        jnp.where((rel == row_ids + k * TR) & live, 1.0, 0.0).astype(BF16) for k in range(3)
    ]
    wt[...] = w[...].T
    bias_t = jnp.broadcast_to(bias[...], (T, W * COLS)).T

    own_ft.wait()
    to_prev.wait_recv()
    to_next.wait_recv()

    for k in range(3):
        for b in range(TR):
            cols3[k * TR + b] = win[k, :, b * T : (b + 1) * T]

    def forward(i, _):
        for u in range(UNROLL):
            s = i * UNROLL + u
            col = cols_s[g, s]
            grp = jnp.minimum(lax.rem(lax.div(col, TR) - g + (ROWS + 1), ROWS), 2)
            p = dot(cols3[grp * TR + lax.rem(col, TR)], tvv[s], NT)
            prods[pl.ds(pl.multiple_of(s * W, W), W), :] = p
        return 0

    for k in range(CHUNKS):
        tile_copies[k].wait()
        lax.fori_loop(k * step // UNROLL, (k + 1) * step // UNROLL, forward, 0)
    select_sum(by_row, prods, TR, sums)
    agg_send[...] = sums[0 : TR * W, :].astype(BF16).reshape(TR, W, T)
    for c in col_peers:
        send(agg_send.at[c], agg_buf.at[me], ss.at[1], rs.at[1], (g, c))
    agg_buf[pl.ds(me, 1)] = agg_send[pl.ds(me, 1)]
    await_blocks(cot_buf, COLS - 1, rs.at[0])
    own_ct.wait()
    await_blocks(agg_buf, COLS - 1, rs.at[1])

    agg_t = agg_buf[...].reshape(COLS * W, T)
    pre = dot(wt[...], agg_t) + bias_t
    sigma = jax.nn.sigmoid(pre)
    cot = cot_buf[...].reshape(COLS * W, T).astype(F32)
    hg = (cot * sigma * (1.0 + pre * (1.0 - sigma))).astype(BF16)
    ag_send[...] = dot(w[...], hg).astype(BF16).reshape(COLS, W, T)
    for c in col_peers:
        send(ag_send.at[c], ag_buf.at[me], ss.at[2], rs.at[2], (g, c))
    ag_buf[pl.ds(me, 1)] = ag_send[pl.ds(me, 1)]
    act_send[...] = (pre * sigma).astype(BF16).reshape(COLS, W, T)
    for c in col_peers:
        send(act_send.at[c], act_buf.at[me], ss.at[3], rs.at[3], (g, c))
    act_buf[pl.ds(me, 1)] = act_send[pl.ds(me, 1)]

    s1_send[:, :, 0 : COLS * W] = dot(agg_t, hg, NT).reshape(32, 8, COLS * W)
    bias_rows = dot(jnp.ones((8, T), BF16), hg, NT)
    bias_tile = jnp.where(
        lax.broadcasted_iota(jnp.int32, (8, 128), 0) < 4, bias_rows[:, 0:128], bias_rows[:, 128:256]
    )
    s1_send[:, :, COLS * W :] = jnp.broadcast_to(bias_tile[None], (32, 8, 128))
    for r, c, part in z_peers:
        send(s1_send.at[part], s1_buf.at[my_rank], ss.at[4], rs.at[4], (r, c))
    s1_buf[pl.ds(my_rank, 1)] = s1_send[pl.ds(my_part, 1)]

    def exchange(value, send_buf, buf, mine, peers, n):
        send_buf[...] = value
        for peer in peers:
            send(send_buf, buf.at[mine], ss.at[n], rs.at[n], peer)
        buf[pl.ds(mine, 1)] = value[None]

    def total(buf, count, n):
        await_blocks(buf, count - 1, rs.at[n])
        return jnp.sum(buf[...], axis=0)

    exchange(total(s1_buf, 32, 4), r1_send, r1_buf, zb, b_peers, 5)

    def backward(i, _):
        for u in range(UNROLL):
            s = i * UNROLL + u
            p = dot(ag_buf[rows_s[g, s]], tvv[s])
            prods[pl.ds(pl.multiple_of(s * W, W), W), :] = p
        return 0

    await_blocks(ag_buf, COLS - 1, rs.at[2])
    lax.fori_loop(0, slots // UNROLL // 2, backward, 0)
    exchange(total(r1_buf, 4, 5), r2_send, r2_buf, za, a_peers, 6)
    lax.fori_loop(slots // UNROLL // 2, slots // UNROLL, backward, 0)
    back = []
    for k, peer in ((0, prev), (2, nxt)):
        select_sum(by_col[k], prods, TR, sums)
        halo_send[k // 2] = sums[0 : TR * W, :].astype(BF16).reshape(TR, W, T)
        back.append(
            send(
                halo_send.at[k // 2],
                halo_buf.at[k // 2],
                back_ss.at[k // 2],
                back_rs.at[k // 2],
                (peer, me),
            )
        )
    select_sum(by_col[1], prods, TR, sums)
    exchange(total(r2_buf, 4, 6), r3_send, r3_buf, zh, h_peers, 7)

    await_blocks(act_buf, COLS - 1, rs.at[3])
    for k in range(COLS):
        act_o[:, k * T : (k + 1) * T] = act_buf[k]
    for copy in back:
        copy.wait_recv()
    for k in range(COLS):
        fg_o[:, k * T : (k + 1) * T] = (
            sums[k * W : (k + 1) * W, :] + halo_buf[0, k].astype(F32) + halo_buf[1, k].astype(F32)
        ).astype(BF16)
    exchange(total(r3_buf, 2, 7), y_send, y_buf, y, y_peers, 8)
    await_blocks(y_buf, 3, rs.at[8])
    wg_o[0:8, :] = y_buf[2 * zh, :, 0 : COLS * W] * scale
    wg_o[8:16, :] = y_buf[2 * zh + 1, :, 0 : COLS * W] * scale
    tile = y_buf[y, :, COLS * W :]
    row = jnp.where(me < 8, tile[0:1, :], tile[4:5, :]) * scale
    bg_o[...] = pltpu.roll(row, (128 - (me % 8) * W) % 128, 1)[:, 0:W]

    to_prev.wait_send()
    to_next.wait_send()
    for copy in back:
        copy.wait_send()
    for n, buf in ((0, cot_buf), (1, agg_buf), (2, ag_buf), (3, act_buf)):
        await_blocks(buf, COLS - 1, ss.at[n])
    await_blocks(s1_buf, 31, ss.at[4])
    await_blocks(r1_buf, 3, ss.at[5])
    await_blocks(r2_buf, 3, ss.at[6])
    await_blocks(r3_buf, 1, ss.at[7])
    await_blocks(y_buf, 3, ss.at[8])


def on_device(features, tile_values, tile_rows, tile_cols, tile_count, weight, out_bias, cotangent):
    slots = tile_values.shape[1]
    nodes = features.shape[0]
    width = weight.shape[0]
    scale = 1.0 / math.sqrt(nodes * ROWS)
    vmem = pl.BlockSpec(memory_space=pltpu.VMEM)
    hbm = pl.BlockSpec(memory_space=pltpu.HBM)
    blocks = pltpu.VMEM((COLS, W, T), BF16)
    parts = lambda n: pltpu.VMEM((n, 8, width + 128), F32)
    part = pltpu.VMEM((8, width + 128), F32)
    act, fg, wg, bg = pl.pallas_call(
        functools.partial(kernel, slots, scale),
        out_shape=(
            jax.ShapeDtypeStruct((W, nodes), BF16),
            jax.ShapeDtypeStruct((W, nodes), BF16),
            jax.ShapeDtypeStruct((W, width), F32),
            jax.ShapeDtypeStruct((1, W), F32),
        ),
        in_specs=[hbm] * 8,
        out_specs=(vmem,) * 4,
        scratch_shapes=[
            pltpu.SMEM(tile_rows.shape, jnp.int32),
            pltpu.SMEM(tile_cols.shape, jnp.int32),
            pltpu.SMEM(tile_count.shape, jnp.int32),
            pltpu.VMEM(tile_rows.shape, jnp.int32),
            pltpu.VMEM(tile_cols.shape, jnp.int32),
            pltpu.VMEM(weight.shape, BF16),
            pltpu.VMEM((1, width), F32),
            pltpu.VMEM((3, W, nodes), BF16),
            pltpu.VMEM((3 * TR, W, T), BF16),
            pltpu.VMEM((slots, T, T), BF16),
            pltpu.VMEM((slots * W, T), F32),
            pltpu.VMEM((TR * W, T), F32),
            pltpu.VMEM((width, width), BF16),
            blocks,
            blocks,
            blocks,
            blocks,
            blocks,
            blocks,
            blocks,
            pltpu.VMEM((2, TR, W, T), BF16),
            pltpu.VMEM((2, TR, W, T), BF16),
            parts(32),
            parts(32),
            part,
            parts(4),
            part,
            parts(4),
            part,
            parts(2),
            part,
            parts(4),
            pltpu.SemaphoreType.DMA((CHUNKS,)),
            pltpu.SemaphoreType.DMA((9,)),
            pltpu.SemaphoreType.DMA((2,)),
            pltpu.SemaphoreType.DMA((2,)),
            pltpu.SemaphoreType.DMA((2,)),
            pltpu.SemaphoreType.DMA((2,)),
            pltpu.SemaphoreType.DMA((9,)),
            pltpu.SemaphoreType.DMA((9,)),
        ],
        compiler_params=pltpu.CompilerParams(
            collective_id=0, has_side_effects=True, vmem_limit_bytes=56 * 1024 * 1024
        ),
        name="graph_layer",
    )(
        features.T,
        cotangent.T,
        tile_values,
        tile_rows,
        tile_cols,
        tile_count,
        weight,
        out_bias.reshape(1, width),
    )
    return act.T, fg.T, wg, bg.reshape(W)


def solution(mesh):
    in_specs = (
        P("row", "col"),
        P("row", None, None, None),
        P(),
        P(),
        P(),
        P(),
        P(),
        P("row", "col"),
    )
    out_specs = (P("row", "col"), P("row", "col"), P("col", None), P("col"))
    return jax.shard_map(
        on_device, mesh=mesh, in_specs=in_specs, out_specs=out_specs, check_vma=False
    )
```

time: 1180 us -> 111 us (0.09)
  the two profiles are of different devices: /device:TPU:2 before, /device:TPU:96 now
where the time goes in v1:
time: 111 us
  Pallas kernels  104 us (94%)
  local copies, waits for them, and re-layouts  5.43 us (5%)
    pallas_call x1, Pallas kernels, on_device(): pl.pallas_call(functools.partial(kernel, slots, scale), out_shape=(jax.Sh...  104 us
    unnamed x4, local copies, waits for them, and re-layouts  5.43 us

profile of v1, /device:TPU:96, one launch (start us, length us, event | category | flops | bytes accessed | tf_op | source)
XLA Modules:
  0.0 110.5 jit_solution(13637385654280696401)
XLA Ops:
  0.6 104.5 %graph_layer.1 = (bf16[16,2048]{1,0:T(8,128)(2,1)}, bf16[16,2048]{1,0:T(8,128)(2,1)}, f32[16,256]{1,0:T(8,128)}, f32[1,16]{1,0:T(1,128)}) custom-call(bf16[16,2048]{1,0:T(8,128)(2,1)} %bitcast.6, bf16[16,2048]{1,0:T(8,128)(2,1)} %bitcast.7, bf16[1,192,128,128]{3,2,1,0:T(8,128)(2,1)} %tv.1, s32[64,192]{1,0:T(8,128)} %rows_h.1, s32[64,192]{1,0:T(8,128)} %cols_h.1, ...), custom_call_target="tpu_custom_call" | custom-call | tf_op jit(solution)/shard_map/graph_layer/pallas_call | solution.py:341
  105.1 1.5 %copy.16 = bf16[2048,16]{0,1:T(8,128)(2,1)} copy(bf16[2048,16]{0,1:T(8,128)(2,1)} %bitcast.9) | data formatting | bytes 131072
  106.6 1.5 %copy.17 = bf16[2048,16]{0,1:T(8,128)(2,1)} copy(bf16[2048,16]{0,1:T(8,128)(2,1)} %bitcast.8) | data formatting | bytes 131072
  108.1 1.3 %copy.18 = f32[16,256]{1,0:T(8,128)} copy(f32[16,256]{1,0:T(8,128)} %get-tuple-element.18) | data formatting | bytes 32768
  109.4 1.2 %copy.19 = f32[16]{0:T(128)} copy(f32[16]{0:T(128)} %bitcast.11) | data formatting | bytes 128

commit v2 on v1

v2 whole, which is shorter than its diff:
```python
import functools
import math

import jax
import jax.numpy as jnp
from jax import lax
from jax.experimental import pallas as pl
from jax.experimental.pallas import tpu as pltpu
from jax.sharding import PartitionSpec as P

MESH = pl.DeviceIdType.MESH
F32 = jnp.float32
BF16 = jnp.bfloat16
T = 128
TR = 16
W = 16
W2 = 2 * W
ROWS = 64
COLS = 16
UNROLL = 16
CHUNKS = 4
NT = (((1,), (1,)), ((), ()))
NN = (((1,), (0,)), ((), ()))


def dot(a, b, dims=NN):
    return lax.dot_general(a, b, dims, preferred_element_type=F32)


def select_sum(onehot, prods, stride, first, count, targets, out):
    slots = onehot.shape[1]
    for f in range(count):
        v = prods[pl.ds(first + f, slots, stride=stride), :]
        hi = v.astype(BF16)
        lo = (v - hi.astype(F32)).astype(BF16)
        out[pl.ds(f, targets, stride=count), :] = dot(onehot, hi) + dot(onehot, lo)


def kernel(
    slots,
    scale,
    ft,
    ct,
    tv,
    rows_h,
    cols_h,
    count_h,
    w_h,
    bias_h,
    act_o,
    fg_o,
    wg_o,
    bg_o,
    rows_s,
    cols_s,
    count_s,
    rows_v,
    cols_v,
    w,
    bias,
    win,
    cols3,
    tvv,
    prods,
    sums,
    wt,
    bias_t,
    cot_far,
    cot_buf,
    agg_send,
    agg_buf,
    ag_send,
    ag_buf,
    act_full,
    act_buf,
    halo_send,
    halo_buf,
    s1_send,
    s1_buf,
    r1_send,
    r1_buf,
    r2_send,
    r2_buf,
    y_send,
    y_buf,
    tile_sem,
    own_sem,
    halo_ss,
    halo_rs,
    far_ss,
    far_rs,
    back_ss,
    back_rs,
    ss,
    rs,
):
    g = lax.axis_index("row")
    me = lax.axis_index("col")
    z_lo, y = g // 4, g % 4
    za, zb = z_lo // 4, z_lo % 4
    x, zh, core = me // 4, (me // 2) % 2, me % 2
    n = x * 2 + core
    other = (zh + 1) % 2
    mate = x * 4 + other * 2 + core
    z_prev, z_next = (zh + (ROWS - g) // ROWS) % 2, (zh + (g + 1) // ROWS) % 2
    prev = ((g + ROWS - 1) % ROWS, x * 4 + z_prev * 2 + core)
    nxt = ((g + 1) % ROWS, x * 4 + z_next * 2 + core)

    near = []
    plane = []
    for dx in (2, 1, 3, 0):
        for dy in (2, 1, 3, 0):
            for dc in (0, 1):
                px, py, pc = (x + dx) % 4, (y + dy) % 4, (core + dc) % 2
                if (dx, dy, dc) != (0, 0, 0):
                    device = (z_lo * 4 + py, px * 4 + zh * 2 + pc)
                    plane.append((device, (px * 2 + pc) * 4 + py))
                    if dy == 0:
                        near.append((device, px * 2 + pc))
    b_peers = [((za * 4 + (zb + d) % 4) * 4 + y, me) for d in (1, 2, 3)]
    a_peers = [((((za + d) % 4) * 4 + zb) * 4 + y, me) for d in (2, 1, 3)]
    y_peers = [(z_lo * 4 + (y + d) % 4, me) for d in (1, 2, 3)]

    def wide(k):
        return pl.ds(pl.multiple_of(k * 2 * T, 2 * T), 2 * T)

    barrier = pltpu.get_barrier_semaphore()
    everyone = [(g, mate), prev, nxt] + a_peers + b_peers + [device for device, _ in plane]
    for peer in everyone:
        pl.semaphore_signal(barrier, inc=1, device_id=peer, device_id_type=MESH)

    step = slots // CHUNKS
    local = [
        pltpu.make_async_copy(src, dst, own_sem.at[k])
        for k, (src, dst) in enumerate(
            (
                (ft, win.at[zh, 1]),
                (ct.at[:, wide(n)], cot_buf.at[me]),
                (cols_h, cols_s),
                (rows_h, rows_s),
                (cols_h, cols_v),
                (rows_h, rows_v),
                (count_h, count_s),
                (w_h, w),
                (bias_h, bias),
            )
        )
    ] + [
        pltpu.make_async_copy(
            tv.at[0, pl.ds(k * step, step)], tvv.at[pl.ds(k * step, step)], tile_sem.at[k]
        )
        for k in range(CHUNKS)
    ]
    for copy in local:
        copy.start()
    for copy in local:
        copy.wait()

    count = count_s[g]
    live = lax.broadcasted_iota(jnp.int32, (TR, slots), 1) < count
    row_ids = lax.broadcasted_iota(jnp.int32, (TR, slots), 0)
    by_row = jnp.where((rows_v[pl.ds(g, 1), :] == row_ids) & live, 1.0, 0.0).astype(BF16)
    own_cols = cols_v[pl.ds(g, 1), :]
    rel = ((lax.div(own_cols, TR) - g + (ROWS + 1)) % ROWS) * TR + lax.rem(own_cols, TR)
    by_col = [
        jnp.where((rel == row_ids + k * TR) & live, 1.0, 0.0).astype(BF16) for k in range(3)
    ]
    wt[...] = w[...].T
    bias_t[...] = jnp.broadcast_to(bias[...], (2 * T, W * COLS)).T

    pl.semaphore_wait(barrier, len(everyone))

    def send(src, dst, send_sem, recv_sem, peer):
        copy = pltpu.make_async_remote_copy(
            src_ref=src,
            dst_ref=dst,
            send_sem=send_sem,
            recv_sem=recv_sem,
            device_id=peer,
            device_id_type=MESH,
        )
        copy.start()
        return copy

    def await_bytes(view, sem):
        pltpu.make_async_copy(view, view, sem).wait()

    far_ft = send(ft, win.at[zh, 1], far_ss.at[0], far_rs.at[0], (g, mate))
    far_ct = send(ct, cot_far, far_ss.at[1], far_rs.at[1], (g, mate))

    def to_sides(src, half):
        send(src, win.at[half, 0], halo_ss.at[half], halo_rs.at[half], nxt)
        send(src, win.at[half, 2], halo_ss.at[2 + half], halo_rs.at[2 + half], prev)

    to_sides(ft, zh)
    for device, k in near:
        send(ct.at[:, wide(k)], cot_buf.at[me], ss.at[0], rs.at[0], device)
    far_ft.wait_recv()
    to_sides(win.at[other, 1], other)
    far_ct.wait_recv()
    own_cot = pltpu.make_async_copy(cot_far.at[:, wide(n)], cot_buf.at[mate], own_sem.at[1])
    own_cot.start()
    for device, k in near:
        send(cot_far.at[:, wide(k)], cot_buf.at[mate], ss.at[1], rs.at[1], device)

    for k in range(4):
        await_bytes(win.at[0, 0], halo_rs.at[k])
    for h in range(2):
        for k in range(3):
            for b in range(TR):
                cols3[k * TR + b, h * W : (h + 1) * W] = win[h, k, :, b * T : (b + 1) * T]

    def forward(i, _):
        for u in range(UNROLL):
            s = i * UNROLL + u
            col = cols_s[g, s]
            grp = jnp.minimum(lax.rem(lax.div(col, TR) - g + (ROWS + 1), ROWS), 2)
            p = dot(cols3[grp * TR + lax.rem(col, TR)], tvv[s], NT)
            prods[pl.ds(pl.multiple_of(s * W2, W2), W2), :] = p
        return 0

    lax.fori_loop(0, slots // UNROLL, forward, 0)
    select_sum(by_row, prods, W2, 0, W2, TR, sums)
    for r in range(TR):
        for h in range(2):
            first = r * W2 + h * W
            agg_send[r // 2, h, r % 2] = sums[first : first + W, :].astype(BF16)
    for device, k in near:
        send(agg_send.at[k], agg_buf.at[x, :, core], ss.at[2], rs.at[2], device)
    own_agg = pltpu.make_async_copy(agg_send.at[n], agg_buf.at[x, :, core], own_sem.at[2])
    own_agg.start()
    await_bytes(cot_buf.at[pl.ds(0, 7)], rs.at[0])
    await_bytes(cot_buf.at[pl.ds(0, 7)], rs.at[1])
    own_cot.wait()
    own_agg.wait()
    await_bytes(agg_send.at[pl.ds(0, 7)], rs.at[2])

    agg_t = jnp.concatenate(
        [agg_buf[:, :, :, t].reshape(COLS * W, T) for t in range(2)], axis=1
    )
    pre = dot(wt[...], agg_t) + bias_t[...]
    sigma = jax.nn.sigmoid(pre)
    cot = cot_buf[...].reshape(COLS * W, 2 * T).astype(F32)
    hg = (cot * sigma * (1.0 + pre * (1.0 - sigma))).astype(BF16)
    ag = dot(w[...], hg).astype(BF16)
    for k in range(8):
        for h in range(2):
            first = ((k // 2) * 4 + h * 2 + k % 2) * W
            for t in range(2):
                ag_send[k, t, h] = ag[first : first + W, t * T : (t + 1) * T]
    for device, k in near:
        send(ag_send.at[k], ag_buf.at[pl.ds(2 * n, 2)], ss.at[3], rs.at[3], device)
    own_ag = pltpu.make_async_copy(ag_send.at[n], ag_buf.at[pl.ds(2 * n, 2)], own_sem.at[3])
    own_ag.start()

    agg_half = jnp.concatenate(
        [agg_buf[:, pl.ds(zh, 1), :, t].reshape(COLS * W // 2, T) for t in range(2)], axis=1
    )
    wg = dot(agg_half, hg, NT)
    for k in range(8):
        for j in range(4):
            first = k * W + (j // 2) * 8
            s1_send[k * 4 + j, 0] = wg[first : first + 8, (j % 2) * T : (j % 2 + 1) * T]
    bias_rows = dot(jnp.ones((8, 2 * T), BF16), hg, NT)
    bias_tile = jnp.where(
        lax.broadcasted_iota(jnp.int32, (8, 128), 0) < 4, bias_rows[:, 0:128], bias_rows[:, 128:256]
    )
    for k in range(32):
        s1_send[k, 1] = bias_tile
    for device, k in plane:
        send(s1_send.at[k], s1_buf.at[n * 4 + y], ss.at[5], rs.at[5], device)
    s1_buf[pl.ds(n * 4 + y, 1)] = s1_send[pl.ds(n * 4 + y, 1)]
    act_full[...] = (pre * sigma).astype(BF16).reshape(COLS, W, 2 * T)
    for device, k in near:
        send(act_full.at[device[1]], act_buf.at[n], ss.at[4], rs.at[4], device)
    act_buf[pl.ds(n, 1)] = act_full[pl.ds(me, 1)]

    def exchange(value, send_buf, buf, mine, peers, k):
        send_buf[...] = value
        for peer in peers:
            send(send_buf, buf.at[mine], ss.at[k], rs.at[k], peer)
        buf[pl.ds(mine, 1)] = value[None]

    def total(buf, others, k):
        await_bytes(buf.at[pl.ds(0, others)], rs.at[k])
        return jnp.sum(buf[...], axis=0)

    def backward(i, _):
        for u in range(UNROLL):
            s = i * UNROLL + u
            p = dot(ag_buf[rows_s[g, s]].reshape(W2, T), tvv[s])
            prods[pl.ds(pl.multiple_of(s * W2, W2), W2), :] = p
        return 0

    await_bytes(ag_send.at[pl.ds(0, 7)], rs.at[3])
    own_ag.wait()
    turns = slots // UNROLL
    lax.fori_loop(0, turns // 3, backward, 0)
    exchange(total(s1_buf, 31, 5), r1_send, r1_buf, zb, b_peers, 6)
    lax.fori_loop(turns // 3, turns, backward, 0)
    exchange(total(r1_buf, 3, 6), r2_send, r2_buf, za, a_peers, 7)
    back = []
    for k, (peer, half) in enumerate(((prev, z_prev), (nxt, z_next))):
        select_sum(by_col[2 * k], prods, W2, half * W, W, TR, sums)
        halo_send[k] = sums[0 : TR * W, :].astype(BF16).reshape(TR, W, T)
        back.append(send(halo_send.at[k], halo_buf.at[k], back_ss.at[k], back_rs.at[k], peer))
    select_sum(by_col[1], prods, W2, zh * W, W, TR, sums)

    await_bytes(act_buf.at[pl.ds(0, 7)], rs.at[4])
    for k in range(8):
        act_o[:, k * 2 * T : (k + 1) * 2 * T] = act_buf[k]
    for copy in back:
        copy.wait_recv()
    for k in range(TR):
        fg_o[:, k * T : (k + 1) * T] = (
            sums[k * W : (k + 1) * W, :] + halo_buf[0, k].astype(F32) + halo_buf[1, k].astype(F32)
        ).astype(BF16)
    exchange(total(r2_buf, 3, 7), y_send, y_buf, y, y_peers, 8)

    far_ft.wait_send()
    far_ct.wait_send()
    for k in range(4):
        await_bytes(win.at[0, 0], halo_ss.at[k])
    for copy in back:
        copy.wait_send()
    for k, view in (
        (0, cot_buf.at[pl.ds(0, 7)]),
        (1, cot_buf.at[pl.ds(0, 7)]),
        (2, agg_send.at[pl.ds(0, 7)]),
        (3, ag_send.at[pl.ds(0, 7)]),
        (4, act_buf.at[pl.ds(0, 7)]),
        (5, s1_buf.at[pl.ds(0, 31)]),
        (6, r1_buf.at[pl.ds(0, 3)]),
        (7, r2_buf.at[pl.ds(0, 3)]),
        (8, y_buf.at[pl.ds(0, 3)]),
    ):
        await_bytes(view, ss.at[k])
    await_bytes(y_buf.at[pl.ds(0, 3)], rs.at[8])
    for j in range(4):
        wg_o[(j // 2) * 8 : (j // 2 + 1) * 8, (j % 2) * T : (j % 2 + 1) * T] = y_buf[j, 0] * scale
    row = jnp.where(me < 8, y_buf[0, 1, 0:1], y_buf[0, 1, 4:5]) * scale
    bg_o[...] = pltpu.roll(row, (128 - (me % 8) * W) % 128, 1)[:, 0:W]


def on_device(features, tile_values, tile_rows, tile_cols, tile_count, weight, out_bias, cotangent):
    slots = tile_values.shape[1]
    nodes = features.shape[0]
    width = weight.shape[0]
    scale = 1.0 / math.sqrt(nodes * ROWS)
    vmem = pl.BlockSpec(memory_space=pltpu.VMEM)
    hbm = pl.BlockSpec(memory_space=pltpu.HBM)
    parts = lambda k: pltpu.VMEM((k, 2, 8, T), F32)
    part = pltpu.VMEM((2, 8, T), F32)
    act, fg, wg, bg = pl.pallas_call(
        functools.partial(kernel, slots, scale),
        out_shape=(
            jax.ShapeDtypeStruct((W, nodes), BF16),
            jax.ShapeDtypeStruct((W, nodes), BF16),
            jax.ShapeDtypeStruct((W, width), F32),
            jax.ShapeDtypeStruct((1, W), F32),
        ),
        in_specs=[hbm] * 8,
        out_specs=(vmem,) * 4,
        scratch_shapes=[
            pltpu.SMEM(tile_rows.shape, jnp.int32),
            pltpu.SMEM(tile_cols.shape, jnp.int32),
            pltpu.SMEM(tile_count.shape, jnp.int32),
            pltpu.VMEM(tile_rows.shape, jnp.int32),
            pltpu.VMEM(tile_cols.shape, jnp.int32),
            pltpu.VMEM(weight.shape, BF16),
            pltpu.VMEM((1, width), F32),
            pltpu.VMEM((2, 3, W, nodes), BF16),
            pltpu.VMEM((3 * TR, W2, T), BF16),
            pltpu.VMEM((slots, T, T), BF16),
            pltpu.VMEM((slots * W2, T), F32),
            pltpu.VMEM((TR * W2, T), F32),
            pltpu.VMEM((width, width), BF16),
            pltpu.VMEM((width, 2 * T), F32),
            pltpu.VMEM((W, nodes), BF16),
            pltpu.VMEM((COLS, W, 2 * T), BF16),
            pltpu.VMEM((8, 2, 2, W, T), BF16),
            pltpu.VMEM((4, 2, 2, 2, W, T), BF16),
            pltpu.VMEM((8, 2, 2, W, T), BF16),
            pltpu.VMEM((TR, 2, W, T), BF16),
            pltpu.VMEM((COLS, W, 2 * T), BF16),
            pltpu.VMEM((8, W, 2 * T), BF16),
            pltpu.VMEM((2, TR, W, T), BF16),
            pltpu.VMEM((2, TR, W, T), BF16),
            parts(32),
            parts(32),
            part,
            parts(4),
            part,
            parts(4),
            part,
            parts(4),
            pltpu.SemaphoreType.DMA((CHUNKS,)),
            pltpu.SemaphoreType.DMA((9,)),
            pltpu.SemaphoreType.DMA((4,)),
            pltpu.SemaphoreType.DMA((4,)),
            pltpu.SemaphoreType.DMA((2,)),
            pltpu.SemaphoreType.DMA((2,)),
            pltpu.SemaphoreType.DMA((2,)),
            pltpu.SemaphoreType.DMA((2,)),
            pltpu.SemaphoreType.DMA((9,)),
            pltpu.SemaphoreType.DMA((9,)),
        ],
        compiler_params=pltpu.CompilerParams(
            collective_id=0, has_side_effects=True, vmem_limit_bytes=32 * 1024 * 1024
        ),
        name="graph_layer",
    )(
        features.T,
        cotangent.T,
        tile_values,
        tile_rows,
        tile_cols,
        tile_count,
        weight,
        out_bias.reshape(1, width),
    )
    return act.T, fg.T, wg, bg.reshape(W)


def solution(mesh):
    in_specs = (
        P("row", "col"),
        P("row", None, None, None),
        P(),
        P(),
        P(),
        P(),
        P(),
        P("row", "col"),
    )
    out_specs = (P("row", "col"), P("row", "col"), P("col", None), P("col"))
    return jax.shard_map(
        on_device, mesh=mesh, in_specs=in_specs, out_specs=out_specs, check_vma=False
    )
```

time: 111 us -> 112 us (level)
  the two profiles are of different devices: /device:TPU:96 before, /device:TPU:1 now
where the time goes in v2:
time: 112 us; the launch traced here: 110 us
  Pallas kernels  98.7 us (88%)
  local copies, waits for them, and re-layouts  10.7 us (10%)
    pallas_call x1, Pallas kernels, on_device(): pl.pallas_call(functools.partial(kernel, slots, scale), out_shape=(jax.Sh...  98.7 us
    unnamed x20, local copies, waits for them, and re-layouts  10.7 us

profile of v2, /device:TPU:1, one launch (start us, length us, event | category | flops | bytes accessed | tf_op | source)
XLA Modules:
  0.0 110.1 jit_solution(7207621280245106258)
XLA Ops:
  0.6 0.0 copy-start
  0.6 2.8 %copy-done = bf16[1,192,128,128]{3,2,1,0:T(8,128)(2,1)S(1)} copy-done((bf16[1,192,128,128]{3,2,1,0:T(8,128)(2,1)S(1)}, bf16[1,192,128,128]{3,2,1,0:T(8,128)(2,1)}, u32[]{:S(2)}) %copy-start) | copy-done | bytes 6291480
  3.4 0.0 copy-start.1
  3.4 0.9 copy-done.1
  4.3 0.0 copy-start.2
  4.3 0.8 copy-done.2
  5.2 0.0 copy-start.3
  5.2 0.8 copy-done.3
  6.0 0.0 copy-start.4
  6.0 0.8 copy-done.4
  6.8 0.0 copy-start.5
  6.8 0.8 copy-done.5
  7.7 0.0 copy-start.6
  7.7 0.7 copy-done.6
  8.4 0.0 copy-start.7
  8.4 0.7 copy-done.7
  9.0 98.7 %graph_layer.1 = (bf16[16,2048]{1,0:T(8,128)(2,1)S(1)}, bf16[16,2048]{1,0:T(8,128)(2,1)S(1)}, f32[16,256]{1,0:T(8,128)S(1)}, f32[1,16]{1,0:T(1,128)S(1)}) custom-call(bf16[16,2048]{1,0:T(8,128)(2,1)S(1)} %bitcast.6, bf16[16,2048]{1,0:T(8,128)(2,1)S(1)} %bitcast.7, bf16[1,192,128,128]{3,2,1,0:T(8,128)(2,1)S(1)} %copy-done, s32[64,192]{1,0:T(8,128)S(1)} %copy-done.4, ...), custom_call_target="tpu_custom_call" | custom-call | tf_op jit(solution)/shard_map/graph_layer/pallas_call | solution.py:354
  107.8 0.6 copy.16
  108.4 0.6 copy.17
  109.0 0.6 copy.18
  109.6 0.5 copy.19
Async XLA Ops:
  0.6 2.8 %copy-start = (bf16[1,192,128,128]{3,2,1,0:T(8,128)(2,1)S(1)}, bf16[1,192,128,128]{3,2,1,0:T(8,128)(2,1)}, u32[]{:S(2)}) copy-start(bf16[1,192,128,128]{3,2,1,0:T(8,128)(2,1)} %tv.1) | copy-start | bytes 18874372
  3.4 0.9 copy-start.1
  4.3 0.8 copy-start.2
  5.2 0.8 copy-start.3
  6.0 0.8 copy-start.4
  6.8 0.8 copy-start.5
  7.7 0.7 copy-start.6
  8.4 0.7 copy-start.7

commit v3 on v2

--- a/solution.py
+++ b/solution.py
@@ -17,7 +17,7 @@
 W2 = 2 * W
 ROWS = 64
 COLS = 16
-UNROLL = 16
+UNROLL = 48
 CHUNKS = 4
 NT = (((1,), (1,)), ((), ()))
 NN = (((1,), (0,)), ((), ()))
@@ -31,9 +31,7 @@
     slots = onehot.shape[1]
     for f in range(count):
         v = prods[pl.ds(first + f, slots, stride=stride), :]
-        hi = v.astype(BF16)
-        lo = (v - hi.astype(F32)).astype(BF16)
-        out[pl.ds(f, targets, stride=count), :] = dot(onehot, hi) + dot(onehot, lo)
+        out[pl.ds(f, targets, stride=count), :] = dot(onehot, v.astype(BF16))
 
 
 def kernel(
@@ -61,6 +59,7 @@
     win,
     cols3,
     tvv,
+    tvt,
     prods,
     sums,
     wt,
@@ -97,7 +96,6 @@
     g = lax.axis_index("row")
     me = lax.axis_index("col")
     z_lo, y = g // 4, g % 4
-    za, zb = z_lo // 4, z_lo % 4
     x, zh, core = me // 4, (me // 2) % 2, me % 2
     n = x * 2 + core
     other = (zh + 1) % 2
@@ -117,17 +115,39 @@
                     plane.append((device, (px * 2 + pc) * 4 + py))
                     if dy == 0:
                         near.append((device, px * 2 + pc))
-    b_peers = [((za * 4 + (zb + d) % 4) * 4 + y, me) for d in (1, 2, 3)]
-    a_peers = [((((za + d) % 4) * 4 + zb) * 4 + y, me) for d in (2, 1, 3)]
+    def along(offset):
+        at = (zh * 16 + z_lo + offset + 32) % 32
+        return ((at % 16) * 4 + y, x * 4 + (at // 16) * 2 + core), at // 16
+
+    near_steps = [(along(-d), d) for d in (1, 2, 3)]
+    wide_steps = [(along(d), k) for k, d in ((1, 8), (2, 4), (3, -4))]
     y_peers = [(z_lo * 4 + (y + d) % 4, me) for d in (1, 2, 3)]
 
     def wide(k):
         return pl.ds(pl.multiple_of(k * 2 * T, 2 * T), 2 * T)
 
     barrier = pltpu.get_barrier_semaphore()
-    everyone = [(g, mate), prev, nxt] + a_peers + b_peers + [device for device, _ in plane]
+    everyone = [(g, mate), prev, nxt]
+    everyone += [along(d)[0] for d in (1, 2, 3, -8, -4, 4)]
+    everyone += [device for device, _ in plane]
     for peer in everyone:
         pl.semaphore_signal(barrier, inc=1, device_id=peer, device_id_type=MESH)
+    pl.semaphore_wait(barrier, len(everyone))
+
+    def send(src, dst, send_sem, recv_sem, peer):
+        copy = pltpu.make_async_remote_copy(
+            src_ref=src,
+            dst_ref=dst,
+            send_sem=send_sem,
+            recv_sem=recv_sem,
+            device_id=peer,
+            device_id_type=MESH,
+        )
+        copy.start()
+        return copy
+
+    def await_bytes(view, sem):
+        pltpu.make_async_copy(view, view, sem).wait()
 
     step = slots // CHUNKS
     local = [
@@ -153,6 +173,27 @@
     ]
     for copy in local:
         copy.start()
+
+    half_nodes = ft.shape[1] // 2
+    pieces = [pl.ds(k * half_nodes, half_nodes) for k in range(2)]
+
+    def to_sides(src, half, piece):
+        there = src.at[:, piece]
+        send(there, win.at[half, 0, :, piece], halo_ss.at[half], halo_rs.at[half], nxt)
+        send(there, win.at[half, 2, :, piece], halo_ss.at[2 + half], halo_rs.at[2 + half], prev)
+
+    far_ft = [
+        send(ft.at[:, piece], win.at[zh, 1, :, piece], far_ss.at[k], far_rs.at[k], (g, mate))
+        for k, piece in enumerate(pieces)
+    ]
+    for piece in pieces:
+        to_sides(ft, zh, piece)
+    for device, k in near:
+        send(ct.at[:, wide(k)], cot_buf.at[me], ss.at[0], rs.at[0], device)
+    for copy in far_ft:
+        copy.wait_send()
+    far_ct = send(ct, cot_far, far_ss.at[2], far_rs.at[2], (g, mate))
+
     for copy in local:
         copy.wait()
 
@@ -168,40 +209,15 @@
     wt[...] = w[...].T
     bias_t[...] = jnp.broadcast_to(bias[...], (2 * T, W * COLS)).T
 
-    pl.semaphore_wait(barrier, len(everyone))
-
-    def send(src, dst, send_sem, recv_sem, peer):
-        copy = pltpu.make_async_remote_copy(
-            src_ref=src,
-            dst_ref=dst,
-            send_sem=send_sem,
-            recv_sem=recv_sem,
-            device_id=peer,
-            device_id_type=MESH,
-        )
-        copy.start()
-        return copy
-
-    def await_bytes(view, sem):
-        pltpu.make_async_copy(view, view, sem).wait()
-
-    far_ft = send(ft, win.at[zh, 1], far_ss.at[0], far_rs.at[0], (g, mate))
-    far_ct = send(ct, cot_far, far_ss.at[1], far_rs.at[1], (g, mate))
-
-    def to_sides(src, half):
-        send(src, win.at[half, 0], halo_ss.at[half], halo_rs.at[half], nxt)
-        send(src, win.at[half, 2], halo_ss.at[2 + half], halo_rs.at[2 + half], prev)
-
-    to_sides(ft, zh)
-    for device, k in near:
-        send(ct.at[:, wide(k)], cot_buf.at[me], ss.at[0], rs.at[0], device)
-    far_ft.wait_recv()
-    to_sides(win.at[other, 1], other)
-    far_ct.wait_recv()
-    own_cot = pltpu.make_async_copy(cot_far.at[:, wide(n)], cot_buf.at[mate], own_sem.at[1])
-    own_cot.start()
-    for device, k in near:
-        send(cot_far.at[:, wide(k)], cot_buf.at[mate], ss.at[1], rs.at[1], device)
+    def turn(i, _):
+        for u in range(8):
+            tvt[i * 8 + u] = tvv[i * 8 + u].T
+        return 0
+
+    lax.fori_loop(0, slots // 8, turn, 0)
+    for k, piece in enumerate(pieces):
+        far_ft[k].wait_recv()
+        to_sides(win.at[other, 1], other, piece)
 
     for k in range(4):
         await_bytes(win.at[0, 0], halo_rs.at[k])
@@ -215,7 +231,7 @@
             s = i * UNROLL + u
             col = cols_s[g, s]
             grp = jnp.minimum(lax.rem(lax.div(col, TR) - g + (ROWS + 1), ROWS), 2)
-            p = dot(cols3[grp * TR + lax.rem(col, TR)], tvv[s], NT)
+            p = dot(cols3[grp * TR + lax.rem(col, TR)], tvt[s])
             prods[pl.ds(pl.multiple_of(s * W2, W2), W2), :] = p
         return 0
 
@@ -227,6 +243,11 @@
             agg_send[r // 2, h, r % 2] = sums[first : first + W, :].astype(BF16)
     for device, k in near:
         send(agg_send.at[k], agg_buf.at[x, :, core], ss.at[2], rs.at[2], device)
+    far_ct.wait_recv()
+    own_cot = pltpu.make_async_copy(cot_far.at[:, wide(n)], cot_buf.at[mate], own_sem.at[1])
+    own_cot.start()
+    for device, k in near:
+        send(cot_far.at[:, wide(k)], cot_buf.at[mate], ss.at[1], rs.at[1], device)
     own_agg = pltpu.make_async_copy(agg_send.at[n], agg_buf.at[x, :, core], own_sem.at[2])
     own_agg.start()
     await_bytes(cot_buf.at[pl.ds(0, 7)], rs.at[0])
@@ -253,20 +274,18 @@
     own_ag = pltpu.make_async_copy(ag_send.at[n], ag_buf.at[pl.ds(2 * n, 2)], own_sem.at[3])
     own_ag.start()
 
-    agg_half = jnp.concatenate(
-        [agg_buf[:, pl.ds(zh, 1), :, t].reshape(COLS * W // 2, T) for t in range(2)], axis=1
-    )
-    wg = dot(agg_half, hg, NT)
+    wg = dot(agg_t, hg, NT)
     for k in range(8):
         for j in range(4):
-            first = k * W + (j // 2) * 8
-            s1_send[k * 4 + j, 0] = wg[first : first + 8, (j % 2) * T : (j % 2 + 1) * T]
+            for h in range(2):
+                first = ((k // 2) * 4 + h * 2 + k % 2) * W + (j // 2) * 8
+                s1_send[k * 4 + j, h] = wg[first : first + 8, (j % 2) * T : (j % 2 + 1) * T]
     bias_rows = dot(jnp.ones((8, 2 * T), BF16), hg, NT)
     bias_tile = jnp.where(
         lax.broadcasted_iota(jnp.int32, (8, 128), 0) < 4, bias_rows[:, 0:128], bias_rows[:, 128:256]
     )
     for k in range(32):
-        s1_send[k, 1] = bias_tile
+        s1_send[k, 2] = bias_tile
     for device, k in plane:
         send(s1_send.at[k], s1_buf.at[n * 4 + y], ss.at[5], rs.at[5], device)
     s1_buf[pl.ds(n * 4 + y, 1)] = s1_send[pl.ds(n * 4 + y, 1)]
@@ -275,15 +294,25 @@
         send(act_full.at[device[1]], act_buf.at[n], ss.at[4], rs.at[4], device)
     act_buf[pl.ds(n, 1)] = act_full[pl.ds(me, 1)]
 
-    def exchange(value, send_buf, buf, mine, peers, k):
-        send_buf[...] = value
-        for peer in peers:
-            send(send_buf, buf.at[mine], ss.at[k], rs.at[k], peer)
-        buf[pl.ds(mine, 1)] = value[None]
-
     def total(buf, others, k):
         await_bytes(buf.at[pl.ds(0, others)], rs.at[k])
         return jnp.sum(buf[...], axis=0)
+
+    def near_sum():
+        value = total(s1_buf, 31, 5)
+        r1_send[...] = value
+        for (device, _), k in near_steps:
+            send(r1_send, r1_buf.at[k - 1], ss.at[6], rs.at[6], device)
+        r1_buf[3] = value
+
+    def wide_sum():
+        value = total(r1_buf, 3, 6)
+        for h in range(2):
+            r2_send[h, 0] = value[h]
+            r2_send[h, 1] = value[2]
+        for (device, half), k in wide_steps:
+            send(r2_send.at[half], r2_buf.at[k - 1], ss.at[7], rs.at[7], device)
+        r2_buf[pl.ds(3, 1)] = r2_send[pl.ds(zh, 1)]
 
     def backward(i, _):
         for u in range(UNROLL):
@@ -295,15 +324,15 @@
     await_bytes(ag_send.at[pl.ds(0, 7)], rs.at[3])
     own_ag.wait()
     turns = slots // UNROLL
-    lax.fori_loop(0, turns // 3, backward, 0)
-    exchange(total(s1_buf, 31, 5), r1_send, r1_buf, zb, b_peers, 6)
-    lax.fori_loop(turns // 3, turns, backward, 0)
-    exchange(total(r1_buf, 3, 6), r2_send, r2_buf, za, a_peers, 7)
+    lax.fori_loop(0, turns // 2, backward, 0)
+    near_sum()
+    lax.fori_loop(turns // 2, turns, backward, 0)
     back = []
     for k, (peer, half) in enumerate(((prev, z_prev), (nxt, z_next))):
         select_sum(by_col[2 * k], prods, W2, half * W, W, TR, sums)
         halo_send[k] = sums[0 : TR * W, :].astype(BF16).reshape(TR, W, T)
         back.append(send(halo_send.at[k], halo_buf.at[k], back_ss.at[k], back_rs.at[k], peer))
+    wide_sum()
     select_sum(by_col[1], prods, W2, zh * W, W, TR, sums)
 
     await_bytes(act_buf.at[pl.ds(0, 7)], rs.at[4])
@@ -315,9 +344,12 @@
         fg_o[:, k * T : (k + 1) * T] = (
             sums[k * W : (k + 1) * W, :] + halo_buf[0, k].astype(F32) + halo_buf[1, k].astype(F32)
         ).astype(BF16)
-    exchange(total(r2_buf, 3, 7), y_send, y_buf, y, y_peers, 8)
-
-    far_ft.wait_send()
+    value = total(r2_buf, 3, 7)
+    y_send[...] = value
+    for device in y_peers:
+        send(y_send, y_buf.at[y], ss.at[8], rs.at[8], device)
+    y_buf[pl.ds(y, 1)] = value[None]
+
     far_ct.wait_send()
     for k in range(4):
         await_bytes(win.at[0, 0], halo_ss.at[k])
@@ -349,8 +381,7 @@
     scale = 1.0 / math.sqrt(nodes * ROWS)
     vmem = pl.BlockSpec(memory_space=pltpu.VMEM)
     hbm = pl.BlockSpec(memory_space=pltpu.HBM)
-    parts = lambda k: pltpu.VMEM((k, 2, 8, T), F32)
-    part = pltpu.VMEM((2, 8, T), F32)
+    tiles = lambda *k: pltpu.VMEM(k + (8, T), F32)
     act, fg, wg, bg = pl.pallas_call(
         functools.partial(kernel, slots, scale),
         out_shape=(
@@ -372,6 +403,7 @@
             pltpu.VMEM((2, 3, W, nodes), BF16),
             pltpu.VMEM((3 * TR, W2, T), BF16),
             pltpu.VMEM((slots, T, T), BF16),
+            pltpu.VMEM((slots, T, T), BF16),
             pltpu.VMEM((slots * W2, T), F32),
             pltpu.VMEM((TR * W2, T), F32),
             pltpu.VMEM((width, width), BF16),
@@ -386,20 +418,20 @@
             pltpu.VMEM((8, W, 2 * T), BF16),
             pltpu.VMEM((2, TR, W, T), BF16),
             pltpu.VMEM((2, TR, W, T), BF16),
-            parts(32),
-            parts(32),
-            part,
-            parts(4),
-            part,
-            parts(4),
-            part,
-            parts(4),
+            tiles(32, 3),
+            tiles(32, 3),
+            tiles(3),
+            tiles(4, 3),
+            tiles(2, 2),
+            tiles(4, 2),
+            tiles(2),
+            tiles(4, 2),
             pltpu.SemaphoreType.DMA((CHUNKS,)),
             pltpu.SemaphoreType.DMA((9,)),
             pltpu.SemaphoreType.DMA((4,)),
             pltpu.SemaphoreType.DMA((4,)),
-            pltpu.SemaphoreType.DMA((2,)),
-            pltpu.SemaphoreType.DMA((2,)),
+            pltpu.SemaphoreType.DMA((3,)),
+            pltpu.SemaphoreType.DMA((3,)),
             pltpu.SemaphoreType.DMA((2,)),
             pltpu.SemaphoreType.DMA((2,)),
             pltpu.SemaphoreType.DMA((9,)),

time: 112 us -> 107 us (0.955)
  the two profiles are of different devices: /device:TPU:1 before, /device:TPU:64 now
where the time goes in v3:
time: 107 us
  Pallas kernels  95.6 us (89%)
  local copies, waits for them, and re-layouts  10.7 us (10%)
    pallas_call x1, Pallas kernels, on_device(): pl.pallas_call(functools.partial(kernel, slots, scale), out_shape=(jax.Sh...  95.6 us
    unnamed x20, local copies, waits for them, and re-layouts  10.7 us

profile of v3, /device:TPU:64, one launch (start us, length us, event | category | flops | bytes accessed | tf_op | source)
XLA Modules:
  0.0 107.0 jit_solution(14348892929182095316)
XLA Ops:
  0.6 0.0 copy-start
  0.6 2.8 %copy-done = bf16[1,192,128,128]{3,2,1,0:T(8,128)(2,1)S(1)} copy-done((bf16[1,192,128,128]{3,2,1,0:T(8,128)(2,1)S(1)}, bf16[1,192,128,128]{3,2,1,0:T(8,128)(2,1)}, u32[]{:S(2)}) %copy-start) | copy-done | bytes 6291480
  3.4 0.0 copy-start.1
  3.4 0.9 copy-done.1
  4.3 0.0 copy-start.2
  4.3 0.8 copy-done.2
  5.2 0.0 copy-start.3
  5.2 0.8 copy-done.3
  6.0 0.0 copy-start.4
  6.0 0.8 copy-done.4
  6.8 0.0 copy-start.5
  6.8 0.8 copy-done.5
  7.7 0.0 copy-start.6
  7.7 0.7 copy-done.6
  8.4 0.0 copy-start.7
  8.4 0.7 copy-done.7
  9.0 95.6 %graph_layer.1 = (bf16[16,2048]{1,0:T(8,128)(2,1)S(1)}, bf16[16,2048]{1,0:T(8,128)(2,1)S(1)}, f32[16,256]{1,0:T(8,128)S(1)}, f32[1,16]{1,0:T(1,128)S(1)}) custom-call(bf16[16,2048]{1,0:T(8,128)(2,1)S(1)} %bitcast.6, bf16[16,2048]{1,0:T(8,128)(2,1)S(1)} %bitcast.7, bf16[1,192,128,128]{3,2,1,0:T(8,128)(2,1)S(1)} %copy-done, s32[64,192]{1,0:T(8,128)S(1)} %copy-done.4, ...), custom_call_target="tpu_custom_call" | custom-call | tf_op jit(solution)/shard_map/graph_layer/pallas_call | solution.py:385
  104.6 0.6 copy.16
  105.2 0.6 copy.17
  105.9 0.6 copy.18
  106.5 0.5 copy.19
Async XLA Ops:
  0.6 2.8 %copy-start = (bf16[1,192,128,128]{3,2,1,0:T(8,128)(2,1)S(1)}, bf16[1,192,128,128]{3,2,1,0:T(8,128)(2,1)}, u32[]{:S(2)}) copy-start(bf16[1,192,128,128]{3,2,1,0:T(8,128)(2,1)} %tv.1) | copy-start | bytes 18874372
  3.4 0.9 copy-start.1
  4.3 0.8 copy-start.2
  5.2 0.8 copy-start.3
  6.0 0.8 copy-start.4
  6.8 0.8 copy-start.5
  7.7 0.7 copy-start.6
  8.4 0.7 copy-start.7

commit v4 on v3

--- a/solution.py
+++ b/solution.py
@@ -31,7 +31,17 @@
     slots = onehot.shape[1]
     for f in range(count):
         v = prods[pl.ds(first + f, slots, stride=stride), :]
-        out[pl.ds(f, targets, stride=count), :] = dot(onehot, v.astype(BF16))
+        hi = v.astype(BF16)
+        lo = (v - hi.astype(F32)).astype(BF16)
+        out[pl.ds(f, targets, stride=count), :] = dot(onehot, hi) + dot(onehot, lo)
+
+
+def two_products(first, second, tiles):
+    none = jnp.zeros_like(first)
+    both = jnp.concatenate(
+        [jnp.concatenate([first, none], axis=1), jnp.concatenate([none, second], axis=1)], axis=0
+    )
+    return dot(both, tiles.reshape(2 * T, T))
 
 
 def kernel(
@@ -190,9 +200,6 @@
         to_sides(ft, zh, piece)
     for device, k in near:
         send(ct.at[:, wide(k)], cot_buf.at[me], ss.at[0], rs.at[0], device)
-    for copy in far_ft:
-        copy.wait_send()
-    far_ct = send(ct, cot_far, far_ss.at[2], far_rs.at[2], (g, mate))
 
     for copy in local:
         copy.wait()
@@ -210,14 +217,18 @@
     bias_t[...] = jnp.broadcast_to(bias[...], (2 * T, W * COLS)).T
 
     def turn(i, _):
-        for u in range(8):
-            tvt[i * 8 + u] = tvv[i * 8 + u].T
+        for u in range(16):
+            tvt[i * 16 + u] = tvv[i * 16 + u].T
         return 0
 
-    lax.fori_loop(0, slots // 8, turn, 0)
+    lax.fori_loop(0, slots // 16, turn, 0)
     for k, piece in enumerate(pieces):
         far_ft[k].wait_recv()
         to_sides(win.at[other, 1], other, piece)
+    far_ct = [
+        send(ct.at[:, piece], cot_far.at[:, piece], far_ss.at[2 + k], far_rs.at[2 + k], (g, mate))
+        for k, piece in enumerate(pieces)
+    ]
 
     for k in range(4):
         await_bytes(win.at[0, 0], halo_rs.at[k])
@@ -226,13 +237,16 @@
             for b in range(TR):
                 cols3[k * TR + b, h * W : (h + 1) * W] = win[h, k, :, b * T : (b + 1) * T]
 
+    def columns_of(s):
+        col = cols_s[g, s]
+        grp = jnp.minimum(lax.rem(lax.div(col, TR) - g + (ROWS + 1), ROWS), 2)
+        return cols3[grp * TR + lax.rem(col, TR)]
+
     def forward(i, _):
-        for u in range(UNROLL):
+        for u in range(0, UNROLL, 2):
             s = i * UNROLL + u
-            col = cols_s[g, s]
-            grp = jnp.minimum(lax.rem(lax.div(col, TR) - g + (ROWS + 1), ROWS), 2)
-            p = dot(cols3[grp * TR + lax.rem(col, TR)], tvt[s])
-            prods[pl.ds(pl.multiple_of(s * W2, W2), W2), :] = p
+            p = two_products(columns_of(s), columns_of(s + 1), tvt[pl.ds(s, 2)])
+            prods[pl.ds(pl.multiple_of(s * W2, 2 * W2), 2 * W2), :] = p
         return 0
 
     lax.fori_loop(0, slots // UNROLL, forward, 0)
@@ -243,7 +257,8 @@
             agg_send[r // 2, h, r % 2] = sums[first : first + W, :].astype(BF16)
     for device, k in near:
         send(agg_send.at[k], agg_buf.at[x, :, core], ss.at[2], rs.at[2], device)
-    far_ct.wait_recv()
+    for copy in far_ct:
+        copy.wait_recv()
     own_cot = pltpu.make_async_copy(cot_far.at[:, wide(n)], cot_buf.at[mate], own_sem.at[1])
     own_cot.start()
     for device, k in near:
@@ -315,10 +330,14 @@
         r2_buf[pl.ds(3, 1)] = r2_send[pl.ds(zh, 1)]
 
     def backward(i, _):
-        for u in range(UNROLL):
+        for u in range(0, UNROLL, 2):
             s = i * UNROLL + u
-            p = dot(ag_buf[rows_s[g, s]].reshape(W2, T), tvv[s])
-            prods[pl.ds(pl.multiple_of(s * W2, W2), W2), :] = p
+            p = two_products(
+                ag_buf[rows_s[g, s]].reshape(W2, T),
+                ag_buf[rows_s[g, s + 1]].reshape(W2, T),
+                tvv[pl.ds(s, 2)],
+            )
+            prods[pl.ds(pl.multiple_of(s * W2, 2 * W2), 2 * W2), :] = p
         return 0
 
     await_bytes(ag_send.at[pl.ds(0, 7)], rs.at[3])
@@ -350,7 +369,8 @@
         send(y_send, y_buf.at[y], ss.at[8], rs.at[8], device)
     y_buf[pl.ds(y, 1)] = value[None]
 
-    far_ct.wait_send()
+    for copy in far_ft + far_ct:
+        copy.wait_send()
     for k in range(4):
         await_bytes(win.at[0, 0], halo_ss.at[k])
     for copy in back:
@@ -430,8 +450,8 @@
             pltpu.SemaphoreType.DMA((9,)),
             pltpu.SemaphoreType.DMA((4,)),
             pltpu.SemaphoreType.DMA((4,)),
-            pltpu.SemaphoreType.DMA((3,)),
-            pltpu.SemaphoreType.DMA((3,)),
+            pltpu.SemaphoreType.DMA((4,)),
+            pltpu.SemaphoreType.DMA((4,)),
             pltpu.SemaphoreType.DMA((2,)),
             pltpu.SemaphoreType.DMA((2,)),
             pltpu.SemaphoreType.DMA((9,)),

time: 107 us -> 107 us (level)
  the two profiles are of different devices: /device:TPU:64 before, /device:TPU:32 now
where the time goes in v4:
time: 107 us; the launch traced here: 106 us
  Pallas kernels  95.1 us (89%)
  local copies, waits for them, and re-layouts  10.7 us (10%)
    pallas_call x1, Pallas kernels, on_device(): pl.pallas_call(functools.partial(kernel, slots, scale), out_shape=(jax.Sh...  95.1 us
    unnamed x20, local copies, waits for them, and re-layouts  10.7 us

profile of v4, /device:TPU:32, one launch (start us, length us, event | category | flops | bytes accessed | tf_op | source)
XLA Modules:
  0.0 106.5 jit_solution(7631862891286815489)
XLA Ops:
  0.6 0.0 copy-start
  0.6 2.8 %copy-done = bf16[1,192,128,128]{3,2,1,0:T(8,128)(2,1)S(1)} copy-done((bf16[1,192,128,128]{3,2,1,0:T(8,128)(2,1)S(1)}, bf16[1,192,128,128]{3,2,1,0:T(8,128)(2,1)}, u32[]{:S(2)}) %copy-start) | copy-done | bytes 6291480
  3.4 0.0 copy-start.1
  3.4 0.9 copy-done.1
  4.3 0.0 copy-start.2
  4.3 0.8 copy-done.2
  5.2 0.0 copy-start.3
  5.2 0.8 copy-done.3
  6.0 0.0 copy-start.4
  6.0 0.8 copy-done.4
  6.8 0.0 copy-start.5
  6.8 0.8 copy-done.5
  7.7 0.0 copy-start.6
  7.7 0.7 copy-done.6
  8.4 0.0 copy-start.7
  8.4 0.7 copy-done.7
  9.0 95.1 %graph_layer.1 = (bf16[16,2048]{1,0:T(8,128)(2,1)S(1)}, bf16[16,2048]{1,0:T(8,128)(2,1)S(1)}, f32[16,256]{1,0:T(8,128)S(1)}, f32[1,16]{1,0:T(1,128)S(1)}) custom-call(bf16[16,2048]{1,0:T(8,128)(2,1)S(1)} %bitcast.6, bf16[16,2048]{1,0:T(8,128)(2,1)S(1)} %bitcast.7, bf16[1,192,128,128]{3,2,1,0:T(8,128)(2,1)S(1)} %copy-done, s32[64,192]{1,0:T(8,128)S(1)} %copy-done.4, ...), custom_call_target="tpu_custom_call" | custom-call | tf_op jit(solution)/shard_map/graph_layer/pallas_call | solution.py:405
  104.1 0.6 copy.16
  104.7 0.6 copy.17
  105.3 0.6 copy.18
  106.0 0.5 copy.19
Async XLA Ops:
  0.6 2.8 %copy-start = (bf16[1,192,128,128]{3,2,1,0:T(8,128)(2,1)S(1)}, bf16[1,192,128,128]{3,2,1,0:T(8,128)(2,1)}, u32[]{:S(2)}) copy-start(bf16[1,192,128,128]{3,2,1,0:T(8,128)(2,1)} %tv.1) | copy-start | bytes 18874372
  3.4 0.9 copy-start.1
  4.3 0.8 copy-start.2
  5.2 0.8 copy-start.3
  6.0 0.8 copy-start.4
  6.8 0.8 copy-start.5
  7.7 0.7 copy-start.6
  8.4 0.7 copy-start.7

commit v5 on v4

--- a/solution.py
+++ b/solution.py
@@ -86,6 +86,8 @@
     halo_buf,
     s1_send,
     s1_buf,
+    bias_send,
+    bias_buf,
     r1_send,
     r1_buf,
     r2_send,
@@ -222,13 +224,13 @@
         return 0
 
     lax.fori_loop(0, slots // 16, turn, 0)
-    for k, piece in enumerate(pieces):
-        far_ft[k].wait_recv()
-        to_sides(win.at[other, 1], other, piece)
     far_ct = [
         send(ct.at[:, piece], cot_far.at[:, piece], far_ss.at[2 + k], far_rs.at[2 + k], (g, mate))
         for k, piece in enumerate(pieces)
     ]
+    for k, piece in enumerate(pieces):
+        far_ft[k].wait_recv()
+        to_sides(win.at[other, 1], other, piece)
 
     for k in range(4):
         await_bytes(win.at[0, 0], halo_rs.at[k])
@@ -292,18 +294,22 @@
     wg = dot(agg_t, hg, NT)
     for k in range(8):
         for j in range(4):
-            for h in range(2):
-                first = ((k // 2) * 4 + h * 2 + k % 2) * W + (j // 2) * 8
-                s1_send[k * 4 + j, h] = wg[first : first + 8, (j % 2) * T : (j % 2 + 1) * T]
+            first = ((k // 2) * 4 + k % 2) * W + (j // 2) * 8
+            across = slice((j % 2) * T, (j % 2 + 1) * T)
+            s1_send[k * 4 + j] = jnp.concatenate(
+                [wg[first : first + 8, across], wg[first + 2 * W : first + 2 * W + 8, across]], axis=0
+            ).astype(BF16)
+    for device, k in plane:
+        send(s1_send.at[k], s1_buf.at[n * 4 + y], ss.at[5], rs.at[5], device)
+    s1_buf[pl.ds(n * 4 + y, 1)] = s1_send[pl.ds(n * 4 + y, 1)]
     bias_rows = dot(jnp.ones((8, 2 * T), BF16), hg, NT)
     bias_tile = jnp.where(
         lax.broadcasted_iota(jnp.int32, (8, 128), 0) < 4, bias_rows[:, 0:128], bias_rows[:, 128:256]
     )
-    for k in range(32):
-        s1_send[k, 2] = bias_tile
-    for device, k in plane:
-        send(s1_send.at[k], s1_buf.at[n * 4 + y], ss.at[5], rs.at[5], device)
-    s1_buf[pl.ds(n * 4 + y, 1)] = s1_send[pl.ds(n * 4 + y, 1)]
+    bias_send[...] = bias_tile
+    for device, k in near:
+        send(bias_send, bias_buf.at[n], ss.at[9], rs.at[9], device)
+    bias_buf[pl.ds(n, 1)] = bias_tile[None]
     act_full[...] = (pre * sigma).astype(BF16).reshape(COLS, W, 2 * T)
     for device, k in near:
         send(act_full.at[device[1]], act_buf.at[n], ss.at[4], rs.at[4], device)
@@ -311,10 +317,10 @@
 
     def total(buf, others, k):
         await_bytes(buf.at[pl.ds(0, others)], rs.at[k])
-        return jnp.sum(buf[...], axis=0)
+        return jnp.sum(buf[...].astype(F32), axis=0)
 
     def near_sum():
-        value = total(s1_buf, 31, 5)
+        value = jnp.concatenate([total(s1_buf, 31, 5), total(bias_buf, 7, 9)], axis=0).reshape(3, 8, T)
         r1_send[...] = value
         for (device, _), k in near_steps:
             send(r1_send, r1_buf.at[k - 1], ss.at[6], rs.at[6], device)
@@ -343,15 +349,14 @@
     await_bytes(ag_send.at[pl.ds(0, 7)], rs.at[3])
     own_ag.wait()
     turns = slots // UNROLL
-    lax.fori_loop(0, turns // 2, backward, 0)
     near_sum()
-    lax.fori_loop(turns // 2, turns, backward, 0)
+    lax.fori_loop(0, turns, backward, 0)
+    wide_sum()
     back = []
     for k, (peer, half) in enumerate(((prev, z_prev), (nxt, z_next))):
         select_sum(by_col[2 * k], prods, W2, half * W, W, TR, sums)
         halo_send[k] = sums[0 : TR * W, :].astype(BF16).reshape(TR, W, T)
         back.append(send(halo_send.at[k], halo_buf.at[k], back_ss.at[k], back_rs.at[k], peer))
-    wide_sum()
     select_sum(by_col[1], prods, W2, zh * W, W, TR, sums)
 
     await_bytes(act_buf.at[pl.ds(0, 7)], rs.at[4])
@@ -385,12 +390,14 @@
         (6, r1_buf.at[pl.ds(0, 3)]),
         (7, r2_buf.at[pl.ds(0, 3)]),
         (8, y_buf.at[pl.ds(0, 3)]),
+        (9, bias_buf.at[pl.ds(0, 7)]),
     ):
         await_bytes(view, ss.at[k])
     await_bytes(y_buf.at[pl.ds(0, 3)], rs.at[8])
     for j in range(4):
         wg_o[(j // 2) * 8 : (j // 2 + 1) * 8, (j % 2) * T : (j % 2 + 1) * T] = y_buf[j, 0] * scale
-    row = jnp.where(me < 8, y_buf[0, 1, 0:1], y_buf[0, 1, 4:5]) * scale
+    bias_sum = jnp.sum(y_buf[:, 1], axis=0)
+    row = jnp.where(me < 8, bias_sum[0:1], bias_sum[4:5]) * scale
     bg_o[...] = pltpu.roll(row, (128 - (me % 8) * W) % 128, 1)[:, 0:W]
 
 
@@ -438,8 +445,10 @@
             pltpu.VMEM((8, W, 2 * T), BF16),
             pltpu.VMEM((2, TR, W, T), BF16),
             pltpu.VMEM((2, TR, W, T), BF16),
-            tiles(32, 3),
-            tiles(32, 3),
+            pltpu.VMEM((32, W, T), BF16),
+            pltpu.VMEM((32, W, T), BF16),
+            tiles(),
+            tiles(8),
             tiles(3),
             tiles(4, 3),
             tiles(2, 2),
@@ -454,8 +463,8 @@
             pltpu.SemaphoreType.DMA((4,)),
             pltpu.SemaphoreType.DMA((2,)),
             pltpu.SemaphoreType.DMA((2,)),
-            pltpu.SemaphoreType.DMA((9,)),
-            pltpu.SemaphoreType.DMA((9,)),
+            pltpu.SemaphoreType.DMA((10,)),
+            pltpu.SemaphoreType.DMA((10,)),
         ],
         compiler_params=pltpu.CompilerParams(
             collective_id=0, has_side_effects=True, vmem_limit_bytes=32 * 1024 * 1024

time: 107 us -> 102 us (0.953)
  the two profiles are of different devices: /device:TPU:32 before, /device:TPU:1 now
where the time goes in v5:
time: 102 us; the launch traced here: 100 us
  Pallas kernels  88.8 us (87%)
  local copies, waits for them, and re-layouts  10.7 us (10%)
    pallas_call x1, Pallas kernels, on_device(): pl.pallas_call(functools.partial(kernel, slots, scale), out_shape=(jax.Sh...  88.8 us
    unnamed x20, local copies, waits for them, and re-layouts  10.7 us

profile of v5, /device:TPU:1, one launch (start us, length us, event | category | flops | bytes accessed | tf_op | source)
XLA Modules:
  0.0 100.2 jit_solution(12482825600432226895)
XLA Ops:
  0.6 0.0 copy-start
  0.6 2.8 %copy-done = bf16[1,192,128,128]{3,2,1,0:T(8,128)(2,1)S(1)} copy-done((bf16[1,192,128,128]{3,2,1,0:T(8,128)(2,1)S(1)}, bf16[1,192,128,128]{3,2,1,0:T(8,128)(2,1)}, u32[]{:S(2)}) %copy-start) | copy-done | bytes 6291480
  3.4 0.0 copy-start.1
  3.4 0.9 copy-done.1
  4.3 0.0 copy-start.2
  4.3 0.8 copy-done.2
  5.2 0.0 copy-start.3
  5.2 0.8 copy-done.3
  6.0 0.0 copy-start.4
  6.0 0.8 copy-done.4
  6.8 0.0 copy-start.5
  6.8 0.8 copy-done.5
  7.7 0.0 copy-start.6
  7.7 0.7 copy-done.6
  8.4 0.0 copy-start.7
  8.4 0.7 copy-done.7
  9.0 88.8 %graph_layer.1 = (bf16[16,2048]{1,0:T(8,128)(2,1)S(1)}, bf16[16,2048]{1,0:T(8,128)(2,1)S(1)}, f32[16,256]{1,0:T(8,128)S(1)}, f32[1,16]{1,0:T(1,128)S(1)}) custom-call(bf16[16,2048]{1,0:T(8,128)(2,1)S(1)} %bitcast.6, bf16[16,2048]{1,0:T(8,128)(2,1)S(1)} %bitcast.7, bf16[1,192,128,128]{3,2,1,0:T(8,128)(2,1)S(1)} %copy-done, s32[64,192]{1,0:T(8,128)S(1)} %copy-done.4, ...), custom_call_target="tpu_custom_call" | custom-call | tf_op jit(solution)/shard_map/graph_layer/pallas_call | solution.py:412
  97.8 0.6 copy.16
  98.5 0.6 copy.17
  99.1 0.6 copy.18
  99.7 0.5 copy.19
Async XLA Ops:
  0.6 2.8 %copy-start = (bf16[1,192,128,128]{3,2,1,0:T(8,128)(2,1)S(1)}, bf16[1,192,128,128]{3,2,1,0:T(8,128)(2,1)}, u32[]{:S(2)}) copy-start(bf16[1,192,128,128]{3,2,1,0:T(8,128)(2,1)} %tv.1) | copy-start | bytes 18874372
  3.4 0.9 copy-start.1
  4.3 0.8 copy-start.2
  5.2 0.8 copy-start.3
  6.0 0.8 copy-start.4
  6.8 0.8 copy-start.5
  7.7 0.7 copy-start.6
  8.4 0.7 copy-start.7

commit v6 on v5

--- a/solution.py
+++ b/solution.py
@@ -19,6 +19,7 @@
 COLS = 16
 UNROLL = 48
 CHUNKS = 4
+PIECES = 4
 NT = (((1,), (1,)), ((), ()))
 NN = (((1,), (0,)), ((), ()))
 
@@ -88,10 +89,8 @@
     s1_buf,
     bias_send,
     bias_buf,
-    r1_send,
-    r1_buf,
-    r2_send,
-    r2_buf,
+    ring_send,
+    ring_buf,
     y_send,
     y_buf,
     tile_sem,
@@ -131,8 +130,7 @@
         at = (zh * 16 + z_lo + offset + 32) % 32
         return ((at % 16) * 4 + y, x * 4 + (at // 16) * 2 + core), at // 16
 
-    near_steps = [(along(-d), d) for d in (1, 2, 3)]
-    wide_steps = [(along(d), k) for k, d in ((1, 8), (2, 4), (3, -4))]
+    offsets = (-8, 7, -7, 6, -6, 5, -5, 4, -4, 3, -3, 2, -2, 1, -1)
     y_peers = [(z_lo * 4 + (y + d) % 4, me) for d in (1, 2, 3)]
 
     def wide(k):
@@ -140,7 +138,7 @@
 
     barrier = pltpu.get_barrier_semaphore()
     everyone = [(g, mate), prev, nxt]
-    everyone += [along(d)[0] for d in (1, 2, 3, -8, -4, 4)]
+    everyone += [along(-d)[0] for d in offsets]
     everyone += [device for device, _ in plane]
     for peer in everyone:
         pl.semaphore_signal(barrier, inc=1, device_id=peer, device_id_type=MESH)
@@ -186,8 +184,8 @@
     for copy in local:
         copy.start()
 
-    half_nodes = ft.shape[1] // 2
-    pieces = [pl.ds(k * half_nodes, half_nodes) for k in range(2)]
+    cut = ft.shape[1] // PIECES
+    pieces = [pl.ds(k * cut, cut) for k in range(PIECES)]
 
     def to_sides(src, half, piece):
         there = src.at[:, piece]
@@ -198,8 +196,7 @@
         send(ft.at[:, piece], win.at[zh, 1, :, piece], far_ss.at[k], far_rs.at[k], (g, mate))
         for k, piece in enumerate(pieces)
     ]
-    for piece in pieces:
-        to_sides(ft, zh, piece)
+    to_sides(ft, zh, pl.ds(0, ft.shape[1]))
     for device, k in near:
         send(ct.at[:, wide(k)], cot_buf.at[me], ss.at[0], rs.at[0], device)
 
@@ -224,10 +221,7 @@
         return 0
 
     lax.fori_loop(0, slots // 16, turn, 0)
-    far_ct = [
-        send(ct.at[:, piece], cot_far.at[:, piece], far_ss.at[2 + k], far_rs.at[2 + k], (g, mate))
-        for k, piece in enumerate(pieces)
-    ]
+    far_ct = send(ct, cot_far, far_ss.at[PIECES], far_rs.at[PIECES], (g, mate))
     for k, piece in enumerate(pieces):
         far_ft[k].wait_recv()
         to_sides(win.at[other, 1], other, piece)
@@ -252,15 +246,13 @@
         return 0
 
     lax.fori_loop(0, slots // UNROLL, forward, 0)
-    select_sum(by_row, prods, W2, 0, W2, TR, sums)
-    for r in range(TR):
-        for h in range(2):
-            first = r * W2 + h * W
-            agg_send[r // 2, h, r % 2] = sums[first : first + W, :].astype(BF16)
-    for device, k in near:
-        send(agg_send.at[k], agg_buf.at[x, :, core], ss.at[2], rs.at[2], device)
-    for copy in far_ct:
-        copy.wait_recv()
+    for h in range(2):
+        select_sum(by_row, prods, W2, h * W, W, TR, sums)
+        for r in range(TR):
+            agg_send[r // 2, h, r % 2] = sums[r * W : (r + 1) * W, :].astype(BF16)
+        for device, k in near:
+            send(agg_send.at[k, h], agg_buf.at[x, h, core], ss.at[2], rs.at[2], device)
+    far_ct.wait_recv()
     own_cot = pltpu.make_async_copy(cot_far.at[:, wide(n)], cot_buf.at[mate], own_sem.at[1])
     own_cot.start()
     for device, k in near:
@@ -319,21 +311,17 @@
         await_bytes(buf.at[pl.ds(0, others)], rs.at[k])
         return jnp.sum(buf[...].astype(F32), axis=0)
 
-    def near_sum():
-        value = jnp.concatenate([total(s1_buf, 31, 5), total(bias_buf, 7, 9)], axis=0).reshape(3, 8, T)
-        r1_send[...] = value
-        for (device, _), k in near_steps:
-            send(r1_send, r1_buf.at[k - 1], ss.at[6], rs.at[6], device)
-        r1_buf[3] = value
-
-    def wide_sum():
-        value = total(r1_buf, 3, 6)
+    def ring_sum():
+        plane_sum = total(s1_buf, 31, 5)
+        bias_sum = total(bias_buf, 7, 9)
         for h in range(2):
-            r2_send[h, 0] = value[h]
-            r2_send[h, 1] = value[2]
-        for (device, half), k in wide_steps:
-            send(r2_send.at[half], r2_buf.at[k - 1], ss.at[7], rs.at[7], device)
-        r2_buf[pl.ds(3, 1)] = r2_send[pl.ds(zh, 1)]
+            ring_send[h] = jnp.concatenate(
+                [plane_sum[8 * h : 8 * h + 8], bias_sum], axis=0
+            ).astype(BF16)
+        for d in offsets:
+            device, half = along(d)
+            send(ring_send.at[half], ring_buf.at[d + 8], ss.at[6], rs.at[6], device)
+        ring_buf[pl.ds(8, 1)] = ring_send[pl.ds(zh, 1)]
 
     def backward(i, _):
         for u in range(0, UNROLL, 2):
@@ -349,9 +337,8 @@
     await_bytes(ag_send.at[pl.ds(0, 7)], rs.at[3])
     own_ag.wait()
     turns = slots // UNROLL
-    near_sum()
+    ring_sum()
     lax.fori_loop(0, turns, backward, 0)
-    wide_sum()
     back = []
     for k, (peer, half) in enumerate(((prev, z_prev), (nxt, z_next))):
         select_sum(by_col[2 * k], prods, W2, half * W, W, TR, sums)
@@ -368,13 +355,13 @@
         fg_o[:, k * T : (k + 1) * T] = (
             sums[k * W : (k + 1) * W, :] + halo_buf[0, k].astype(F32) + halo_buf[1, k].astype(F32)
         ).astype(BF16)
-    value = total(r2_buf, 3, 7)
+    value = total(ring_buf, 15, 6).reshape(2, 8, T)
     y_send[...] = value
     for device in y_peers:
         send(y_send, y_buf.at[y], ss.at[8], rs.at[8], device)
     y_buf[pl.ds(y, 1)] = value[None]
 
-    for copy in far_ft + far_ct:
+    for copy in far_ft + [far_ct]:
         copy.wait_send()
     for k in range(4):
         await_bytes(win.at[0, 0], halo_ss.at[k])
@@ -387,8 +374,7 @@
         (3, ag_send.at[pl.ds(0, 7)]),
         (4, act_buf.at[pl.ds(0, 7)]),
         (5, s1_buf.at[pl.ds(0, 31)]),
-        (6, r1_buf.at[pl.ds(0, 3)]),
-        (7, r2_buf.at[pl.ds(0, 3)]),
+        (6, ring_buf.at[pl.ds(0, 15)]),
         (8, y_buf.at[pl.ds(0, 3)]),
         (9, bias_buf.at[pl.ds(0, 7)]),
     ):
@@ -449,18 +435,16 @@
             pltpu.VMEM((32, W, T), BF16),
             tiles(),
             tiles(8),
-            tiles(3),
-            tiles(4, 3),
-            tiles(2, 2),
-            tiles(4, 2),
+            pltpu.VMEM((2, W, T), BF16),
+            pltpu.VMEM((16, W, T), BF16),
             tiles(2),
             tiles(4, 2),
             pltpu.SemaphoreType.DMA((CHUNKS,)),
             pltpu.SemaphoreType.DMA((9,)),
             pltpu.SemaphoreType.DMA((4,)),
             pltpu.SemaphoreType.DMA((4,)),
-            pltpu.SemaphoreType.DMA((4,)),
-            pltpu.SemaphoreType.DMA((4,)),
+            pltpu.SemaphoreType.DMA((PIECES + 1,)),
+            pltpu.SemaphoreType.DMA((PIECES + 1,)),
             pltpu.SemaphoreType.DMA((2,)),
             pltpu.SemaphoreType.DMA((2,)),
             pltpu.SemaphoreType.DMA((10,)),

time: 102 us -> 97.4 us (0.955); the launches traced: 100 us -> 97 us
  Pallas kernels: 88.8 us -> 85.6 us
    pallas_call x1, Pallas kernels: 88.8 us -> 85.6 us  [on_device(): pl.pallas_call(functools.partial(kernel, slots, scale), out_shape=(jax.Sh...]
where the time goes in v6:
time: 97.4 us; the launch traced here: 97 us
  Pallas kernels  85.6 us (88%)
  local copies, waits for them, and re-layouts  10.7 us (11%)
    pallas_call x1, Pallas kernels, on_device(): pl.pallas_call(functools.partial(kernel, slots, scale), out_shape=(jax.Sh...  85.6 us
    unnamed x20, local copies, waits for them, and re-layouts  10.7 us

profile of v6, /device:TPU:1, one launch (start us, length us, event | category | flops | bytes accessed | tf_op | source)
XLA Modules:
  0.0 97.0 jit_solution(11553988542724845623)
XLA Ops:
  0.6 0.0 copy-start
  0.6 2.8 %copy-done = bf16[1,192,128,128]{3,2,1,0:T(8,128)(2,1)S(1)} copy-done((bf16[1,192,128,128]{3,2,1,0:T(8,128)(2,1)S(1)}, bf16[1,192,128,128]{3,2,1,0:T(8,128)(2,1)}, u32[]{:S(2)}) %copy-start) | copy-done | bytes 6291480
  3.4 0.0 copy-start.1
  3.4 0.9 copy-done.1
  4.3 0.0 copy-start.2
  4.3 0.8 copy-done.2
  5.2 0.0 copy-start.3
  5.2 0.8 copy-done.3
  6.0 0.0 copy-start.4
  6.0 0.8 copy-done.4
  6.8 0.0 copy-start.5
  6.8 0.8 copy-done.5
  7.7 0.0 copy-start.6
  7.7 0.7 copy-done.6
  8.4 0.0 copy-start.7
  8.4 0.7 copy-done.7
  9.0 85.6 %graph_layer.1 = (bf16[16,2048]{1,0:T(8,128)(2,1)S(1)}, bf16[16,2048]{1,0:T(8,128)(2,1)S(1)}, f32[16,256]{1,0:T(8,128)S(1)}, f32[1,16]{1,0:T(1,128)S(1)}) custom-call(bf16[16,2048]{1,0:T(8,128)(2,1)S(1)} %bitcast.6, bf16[16,2048]{1,0:T(8,128)(2,1)S(1)} %bitcast.7, bf16[1,192,128,128]{3,2,1,0:T(8,128)(2,1)S(1)} %copy-done, s32[64,192]{1,0:T(8,128)S(1)} %copy-done.4, ...), custom_call_target="tpu_custom_call" | custom-call | tf_op jit(solution)/shard_map/graph_layer/pallas_call | solution.py:398
  94.6 0.6 copy.16
  95.3 0.6 copy.17
  95.9 0.6 copy.18
  96.5 0.5 copy.19
Async XLA Ops:
  0.6 2.8 %copy-start = (bf16[1,192,128,128]{3,2,1,0:T(8,128)(2,1)S(1)}, bf16[1,192,128,128]{3,2,1,0:T(8,128)(2,1)}, u32[]{:S(2)}) copy-start(bf16[1,192,128,128]{3,2,1,0:T(8,128)(2,1)} %tv.1) | copy-start | bytes 18874372
  3.4 0.9 copy-start.1
  4.3 0.8 copy-start.2
  5.2 0.8 copy-start.3
  6.0 0.8 copy-start.4
  6.8 0.8 copy-start.5
  7.7 0.7 copy-start.6
  8.4 0.7 copy-start.7

commit v7 on v6

--- a/solution.py
+++ b/solution.py
@@ -159,6 +159,13 @@
     def await_bytes(view, sem):
         pltpu.make_async_copy(view, view, sem).wait()
 
+    cut = ft.shape[1] // PIECES
+    pieces = [pl.ds(k * cut, cut) for k in range(PIECES)]
+    far_ft = [
+        send(ft.at[:, piece], win.at[zh, 1, :, piece], far_ss.at[k], far_rs.at[k], (g, mate))
+        for k, piece in enumerate(pieces)
+    ]
+
     step = slots // CHUNKS
     local = [
         pltpu.make_async_copy(src, dst, own_sem.at[k])
@@ -184,18 +191,11 @@
     for copy in local:
         copy.start()
 
-    cut = ft.shape[1] // PIECES
-    pieces = [pl.ds(k * cut, cut) for k in range(PIECES)]
-
     def to_sides(src, half, piece):
         there = src.at[:, piece]
         send(there, win.at[half, 0, :, piece], halo_ss.at[half], halo_rs.at[half], nxt)
         send(there, win.at[half, 2, :, piece], halo_ss.at[2 + half], halo_rs.at[2 + half], prev)
 
-    far_ft = [
-        send(ft.at[:, piece], win.at[zh, 1, :, piece], far_ss.at[k], far_rs.at[k], (g, mate))
-        for k, piece in enumerate(pieces)
-    ]
     to_sides(ft, zh, pl.ds(0, ft.shape[1]))
     for device, k in near:
         send(ct.at[:, wide(k)], cot_buf.at[me], ss.at[0], rs.at[0], device)
@@ -246,17 +246,20 @@
         return 0
 
     lax.fori_loop(0, slots // UNROLL, forward, 0)
-    for h in range(2):
+    def sum_rows(h):
         select_sum(by_row, prods, W2, h * W, W, TR, sums)
         for r in range(TR):
             agg_send[r // 2, h, r % 2] = sums[r * W : (r + 1) * W, :].astype(BF16)
         for device, k in near:
             send(agg_send.at[k, h], agg_buf.at[x, h, core], ss.at[2], rs.at[2], device)
+
+    sum_rows(0)
     far_ct.wait_recv()
     own_cot = pltpu.make_async_copy(cot_far.at[:, wide(n)], cot_buf.at[mate], own_sem.at[1])
     own_cot.start()
     for device, k in near:
         send(cot_far.at[:, wide(k)], cot_buf.at[mate], ss.at[1], rs.at[1], device)
+    sum_rows(1)
     own_agg = pltpu.make_async_copy(agg_send.at[n], agg_buf.at[x, :, core], own_sem.at[2])
     own_agg.start()
     await_bytes(cot_buf.at[pl.ds(0, 7)], rs.at[0])
@@ -303,9 +306,6 @@
         send(bias_send, bias_buf.at[n], ss.at[9], rs.at[9], device)
     bias_buf[pl.ds(n, 1)] = bias_tile[None]
     act_full[...] = (pre * sigma).astype(BF16).reshape(COLS, W, 2 * T)
-    for device, k in near:
-        send(act_full.at[device[1]], act_buf.at[n], ss.at[4], rs.at[4], device)
-    act_buf[pl.ds(n, 1)] = act_full[pl.ds(me, 1)]
 
     def total(buf, others, k):
         await_bytes(buf.at[pl.ds(0, others)], rs.at[k])
@@ -344,6 +344,9 @@
         select_sum(by_col[2 * k], prods, W2, half * W, W, TR, sums)
         halo_send[k] = sums[0 : TR * W, :].astype(BF16).reshape(TR, W, T)
         back.append(send(halo_send.at[k], halo_buf.at[k], back_ss.at[k], back_rs.at[k], peer))
+    for device, k in near:
+        send(act_full.at[device[1]], act_buf.at[n], ss.at[4], rs.at[4], device)
+    act_buf[pl.ds(n, 1)] = act_full[pl.ds(me, 1)]
     select_sum(by_col[1], prods, W2, zh * W, W, TR, sums)
 
     await_bytes(act_buf.at[pl.ds(0, 7)], rs.at[4])

time: 97.4 us -> 95.9 us (0.985)
  Pallas kernels: 85.6 us -> 83.8 us
    pallas_call x1, Pallas kernels: 85.6 us -> 83.8 us  [on_device(): pl.pallas_call(functools.partial(kernel, slots, scale), out_shape=(jax.Sh...]
where the time goes in v7:
time: 95.9 us; the launch traced here: 95.2 us
  Pallas kernels  83.8 us (87%)
  local copies, waits for them, and re-layouts  10.7 us (11%)
    pallas_call x1, Pallas kernels, on_device(): pl.pallas_call(functools.partial(kernel, slots, scale), out_shape=(jax.Sh...  83.8 us
    unnamed x20, local copies, waits for them, and re-layouts  10.7 us

profile of v7, /device:TPU:1, one launch (start us, length us, event | category | flops | bytes accessed | tf_op | source)
XLA Modules:
  0.0 95.2 jit_solution(207417857807588995)
XLA Ops:
  0.6 0.0 copy-start
  0.6 2.8 %copy-done = bf16[1,192,128,128]{3,2,1,0:T(8,128)(2,1)S(1)} copy-done((bf16[1,192,128,128]{3,2,1,0:T(8,128)(2,1)S(1)}, bf16[1,192,128,128]{3,2,1,0:T(8,128)(2,1)}, u32[]{:S(2)}) %copy-start) | copy-done | bytes 6291480
  3.4 0.0 copy-start.1
  3.4 0.9 copy-done.1
  4.3 0.0 copy-start.2
  4.3 0.8 copy-done.2
  5.2 0.0 copy-start.3
  5.2 0.8 copy-done.3
  6.0 0.0 copy-start.4
  6.0 0.8 copy-done.4
  6.8 0.0 copy-start.5
  6.8 0.8 copy-done.5
  7.7 0.0 copy-start.6
  7.7 0.7 copy-done.6
  8.4 0.0 copy-start.7
  8.4 0.7 copy-done.7
  9.0 83.8 %graph_layer.1 = (bf16[16,2048]{1,0:T(8,128)(2,1)S(1)}, bf16[16,2048]{1,0:T(8,128)(2,1)S(1)}, f32[16,256]{1,0:T(8,128)S(1)}, f32[1,16]{1,0:T(1,128)S(1)}) custom-call(bf16[16,2048]{1,0:T(8,128)(2,1)S(1)} %bitcast.6, bf16[16,2048]{1,0:T(8,128)(2,1)S(1)} %bitcast.7, bf16[1,192,128,128]{3,2,1,0:T(8,128)(2,1)S(1)} %copy-done, s32[64,192]{1,0:T(8,128)S(1)} %copy-done.4, ...), custom_call_target="tpu_custom_call" | custom-call | tf_op jit(solution)/shard_map/graph_layer/pallas_call | solution.py:401
  92.8 0.6 copy.16
  93.5 0.6 copy.17
  94.1 0.6 copy.18
  94.7 0.5 copy.19
Async XLA Ops:
  0.6 2.8 %copy-start = (bf16[1,192,128,128]{3,2,1,0:T(8,128)(2,1)S(1)}, bf16[1,192,128,128]{3,2,1,0:T(8,128)(2,1)}, u32[]{:S(2)}) copy-start(bf16[1,192,128,128]{3,2,1,0:T(8,128)(2,1)} %tv.1) | copy-start | bytes 18874372
  3.4 0.9 copy-start.1
  4.3 0.8 copy-start.2
  5.2 0.8 copy-start.3
  6.0 0.8 copy-start.4
  6.8 0.8 copy-start.5
  7.7 0.7 copy-start.6
  8.4 0.7 copy-start.7

commit v8 on v6

--- a/solution.py
+++ b/solution.py
@@ -142,23 +142,6 @@
     everyone += [device for device, _ in plane]
     for peer in everyone:
         pl.semaphore_signal(barrier, inc=1, device_id=peer, device_id_type=MESH)
-    pl.semaphore_wait(barrier, len(everyone))
-
-    def send(src, dst, send_sem, recv_sem, peer):
-        copy = pltpu.make_async_remote_copy(
-            src_ref=src,
-            dst_ref=dst,
-            send_sem=send_sem,
-            recv_sem=recv_sem,
-            device_id=peer,
-            device_id_type=MESH,
-        )
-        copy.start()
-        return copy
-
-    def await_bytes(view, sem):
-        pltpu.make_async_copy(view, view, sem).wait()
-
     step = slots // CHUNKS
     local = [
         pltpu.make_async_copy(src, dst, own_sem.at[k])
@@ -183,23 +166,6 @@
     ]
     for copy in local:
         copy.start()
-
-    cut = ft.shape[1] // PIECES
-    pieces = [pl.ds(k * cut, cut) for k in range(PIECES)]
-
-    def to_sides(src, half, piece):
-        there = src.at[:, piece]
-        send(there, win.at[half, 0, :, piece], halo_ss.at[half], halo_rs.at[half], nxt)
-        send(there, win.at[half, 2, :, piece], halo_ss.at[2 + half], halo_rs.at[2 + half], prev)
-
-    far_ft = [
-        send(ft.at[:, piece], win.at[zh, 1, :, piece], far_ss.at[k], far_rs.at[k], (g, mate))
-        for k, piece in enumerate(pieces)
-    ]
-    to_sides(ft, zh, pl.ds(0, ft.shape[1]))
-    for device, k in near:
-        send(ct.at[:, wide(k)], cot_buf.at[me], ss.at[0], rs.at[0], device)
-
     for copy in local:
         copy.wait()
 
@@ -221,6 +187,42 @@
         return 0
 
     lax.fori_loop(0, slots // 16, turn, 0)
+
+    pl.semaphore_wait(barrier, len(everyone))
+
+    def send(src, dst, send_sem, recv_sem, peer):
+        copy = pltpu.make_async_remote_copy(
+            src_ref=src,
+            dst_ref=dst,
+            send_sem=send_sem,
+            recv_sem=recv_sem,
+            device_id=peer,
+            device_id_type=MESH,
+        )
+        copy.start()
+        return copy
+
+    def await_bytes(view, sem):
+        pltpu.make_async_copy(view, view, sem).wait()
+
+    cut = ft.shape[1] // PIECES
+    pieces = [pl.ds(k * cut, cut) for k in range(PIECES)]
+    far_ft = [
+        send(ft.at[:, piece], win.at[zh, 1, :, piece], far_ss.at[k], far_rs.at[k], (g, mate))
+        for k, piece in enumerate(pieces)
+    ]
+
+    def to_sides(src, half, piece):
+        there = src.at[:, piece]
+        send(there, win.at[half, 0, :, piece], halo_ss.at[half], halo_rs.at[half], nxt)
+        send(there, win.at[half, 2, :, piece], halo_ss.at[2 + half], halo_rs.at[2 + half], prev)
+
+    to_sides(ft, zh, pl.ds(0, ft.shape[1]))
+    for device, k in near:
+        send(ct.at[:, wide(k)], cot_buf.at[me], ss.at[0], rs.at[0], device)
+
+    for copy in far_ft:
+        copy.wait_send()
     far_ct = send(ct, cot_far, far_ss.at[PIECES], far_rs.at[PIECES], (g, mate))
     for k, piece in enumerate(pieces):
         far_ft[k].wait_recv()
@@ -246,17 +248,20 @@
         return 0
 
     lax.fori_loop(0, slots // UNROLL, forward, 0)
-    for h in range(2):
+    def sum_rows(h):
         select_sum(by_row, prods, W2, h * W, W, TR, sums)
         for r in range(TR):
             agg_send[r // 2, h, r % 2] = sums[r * W : (r + 1) * W, :].astype(BF16)
         for device, k in near:
             send(agg_send.at[k, h], agg_buf.at[x, h, core], ss.at[2], rs.at[2], device)
+
+    sum_rows(0)
     far_ct.wait_recv()
     own_cot = pltpu.make_async_copy(cot_far.at[:, wide(n)], cot_buf.at[mate], own_sem.at[1])
     own_cot.start()
     for device, k in near:
         send(cot_far.at[:, wide(k)], cot_buf.at[mate], ss.at[1], rs.at[1], device)
+    sum_rows(1)
     own_agg = pltpu.make_async_copy(agg_send.at[n], agg_buf.at[x, :, core], own_sem.at[2])
     own_agg.start()
     await_bytes(cot_buf.at[pl.ds(0, 7)], rs.at[0])
@@ -303,9 +308,6 @@
         send(bias_send, bias_buf.at[n], ss.at[9], rs.at[9], device)
     bias_buf[pl.ds(n, 1)] = bias_tile[None]
     act_full[...] = (pre * sigma).astype(BF16).reshape(COLS, W, 2 * T)
-    for device, k in near:
-        send(act_full.at[device[1]], act_buf.at[n], ss.at[4], rs.at[4], device)
-    act_buf[pl.ds(n, 1)] = act_full[pl.ds(me, 1)]
 
     def total(buf, others, k):
         await_bytes(buf.at[pl.ds(0, others)], rs.at[k])
@@ -344,6 +346,9 @@
         select_sum(by_col[2 * k], prods, W2, half * W, W, TR, sums)
         halo_send[k] = sums[0 : TR * W, :].astype(BF16).reshape(TR, W, T)
         back.append(send(halo_send.at[k], halo_buf.at[k], back_ss.at[k], back_rs.at[k], peer))
+    for device, k in near:
+        send(act_full.at[device[1]], act_buf.at[n], ss.at[4], rs.at[4], device)
+    act_buf[pl.ds(n, 1)] = act_full[pl.ds(me, 1)]
     select_sum(by_col[1], prods, W2, zh * W, W, TR, sums)
 
     await_bytes(act_buf.at[pl.ds(0, 7)], rs.at[4])
@@ -361,8 +366,7 @@
         send(y_send, y_buf.at[y], ss.at[8], rs.at[8], device)
     y_buf[pl.ds(y, 1)] = value[None]
 
-    for copy in far_ft + [far_ct]:
-        copy.wait_send()
+    far_ct.wait_send()
     for k in range(4):
         await_bytes(win.at[0, 0], halo_ss.at[k])
     for copy in back:

time: 97.4 us -> 97.2 us (level)
  no operation moved by 1% of the time
where the time goes in v8:
time: 97.2 us; the launch traced here: 96.8 us
  Pallas kernels  85.4 us (88%)
  local copies, waits for them, and re-layouts  10.7 us (11%)
    pallas_call x1, Pallas kernels, on_device(): pl.pallas_call(functools.partial(kernel, slots, scale), out_shape=(jax.Sh...  85.4 us
    unnamed x20, local copies, waits for them, and re-layouts  10.7 us

profile of v8, /device:TPU:1, one launch (start us, length us, event | category | flops | bytes accessed | tf_op | source)
XLA Modules:
  0.0 96.8 jit_solution(2646686723173256931)
XLA Ops:
  0.6 0.0 copy-start
  0.6 2.8 %copy-done = bf16[1,192,128,128]{3,2,1,0:T(8,128)(2,1)S(1)} copy-done((bf16[1,192,128,128]{3,2,1,0:T(8,128)(2,1)S(1)}, bf16[1,192,128,128]{3,2,1,0:T(8,128)(2,1)}, u32[]{:S(2)}) %copy-start) | copy-done | bytes 6291480
  3.4 0.0 copy-start.1
  3.4 0.9 copy-done.1
  4.3 0.0 copy-start.2
  4.3 0.8 copy-done.2
  5.2 0.0 copy-start.3
  5.2 0.8 copy-done.3
  6.0 0.0 copy-start.4
  6.0 0.8 copy-done.4
  6.8 0.0 copy-start.5
  6.8 0.8 copy-done.5
  7.7 0.0 copy-start.6
  7.7 0.7 copy-done.6
  8.4 0.0 copy-start.7
  8.4 0.7 copy-done.7
  9.0 85.4 %graph_layer.1 = (bf16[16,2048]{1,0:T(8,128)(2,1)S(1)}, bf16[16,2048]{1,0:T(8,128)(2,1)S(1)}, f32[16,256]{1,0:T(8,128)S(1)}, f32[1,16]{1,0:T(1,128)S(1)}) custom-call(bf16[16,2048]{1,0:T(8,128)(2,1)S(1)} %bitcast.6, bf16[16,2048]{1,0:T(8,128)(2,1)S(1)} %bitcast.7, bf16[1,192,128,128]{3,2,1,0:T(8,128)(2,1)S(1)} %copy-done, s32[64,192]{1,0:T(8,128)S(1)} %copy-done.4, ...), custom_call_target="tpu_custom_call" | custom-call | tf_op jit(solution)/shard_map/graph_layer/pallas_call | solution.py:402
  94.4 0.6 copy.16
  95.1 0.6 copy.17
  95.7 0.6 copy.18
  96.3 0.5 copy.19
Async XLA Ops:
  0.6 2.8 %copy-start = (bf16[1,192,128,128]{3,2,1,0:T(8,128)(2,1)S(1)}, bf16[1,192,128,128]{3,2,1,0:T(8,128)(2,1)}, u32[]{:S(2)}) copy-start(bf16[1,192,128,128]{3,2,1,0:T(8,128)(2,1)} %tv.1) | copy-start | bytes 18874372
  3.4 0.9 copy-start.1
  4.3 0.8 copy-start.2
  5.2 0.8 copy-start.3
  6.0 0.8 copy-start.4
  6.8 0.8 copy-start.5
  7.7 0.7 copy-start.6
  8.4 0.7 copy-start.7

commit v9 on v7

--- a/solution.py
+++ b/solution.py
@@ -200,6 +200,10 @@
     for device, k in near:
         send(ct.at[:, wide(k)], cot_buf.at[me], ss.at[0], rs.at[0], device)
 
+    for copy in far_ft:
+        copy.wait_send()
+    far_ct = send(ct, cot_far, far_ss.at[PIECES], far_rs.at[PIECES], (g, mate))
+
     for copy in local:
         copy.wait()
 
@@ -221,7 +225,6 @@
         return 0
 
     lax.fori_loop(0, slots // 16, turn, 0)
-    far_ct = send(ct, cot_far, far_ss.at[PIECES], far_rs.at[PIECES], (g, mate))
     for k, piece in enumerate(pieces):
         far_ft[k].wait_recv()
         to_sides(win.at[other, 1], other, piece)
@@ -364,8 +367,7 @@
         send(y_send, y_buf.at[y], ss.at[8], rs.at[8], device)
     y_buf[pl.ds(y, 1)] = value[None]
 
-    for copy in far_ft + [far_ct]:
-        copy.wait_send()
+    far_ct.wait_send()
     for k in range(4):
         await_bytes(win.at[0, 0], halo_ss.at[k])
     for copy in back:

time: 95.9 us -> 98.8 us (1.030)
  Pallas kernels: 83.8 us -> 86.9 us
    pallas_call x1, Pallas kernels: 83.8 us -> 86.9 us  [on_device(): pl.pallas_call(functools.partial(kernel, slots, scale), out_shape=(jax.Sh...]
where the time goes in v9:
time: 98.8 us; the launch traced here: 98.3 us
  Pallas kernels  86.9 us (88%)
  local copies, waits for them, and re-layouts  10.7 us (11%)
    pallas_call x1, Pallas kernels, on_device(): pl.pallas_call(functools.partial(kernel, slots, scale), out_shape=(jax.Sh...  86.9 us
    unnamed x20, local copies, waits for them, and re-layouts  10.7 us

profile of v9, /device:TPU:1, one launch (start us, length us, event | category | flops | bytes accessed | tf_op | source)
XLA Modules:
  0.0 98.3 jit_solution(485161780037154341)
XLA Ops:
  0.6 0.0 copy-start
  0.6 2.8 %copy-done = bf16[1,192,128,128]{3,2,1,0:T(8,128)(2,1)S(1)} copy-done((bf16[1,192,128,128]{3,2,1,0:T(8,128)(2,1)S(1)}, bf16[1,192,128,128]{3,2,1,0:T(8,128)(2,1)}, u32[]{:S(2)}) %copy-start) | copy-done | bytes 6291480
  3.4 0.0 copy-start.1
  3.4 0.9 copy-done.1
  4.3 0.0 copy-start.2
  4.3 0.8 copy-done.2
  5.2 0.0 copy-start.3
  5.2 0.8 copy-done.3
  6.0 0.0 copy-start.4
  6.0 0.8 copy-done.4
  6.8 0.0 copy-start.5
  6.8 0.8 copy-done.5
  7.7 0.0 copy-start.6
  7.7 0.7 copy-done.6
  8.4 0.0 copy-start.7
  8.4 0.7 copy-done.7
  9.0 86.9 %graph_layer.1 = (bf16[16,2048]{1,0:T(8,128)(2,1)S(1)}, bf16[16,2048]{1,0:T(8,128)(2,1)S(1)}, f32[16,256]{1,0:T(8,128)S(1)}, f32[1,16]{1,0:T(1,128)S(1)}) custom-call(bf16[16,2048]{1,0:T(8,128)(2,1)S(1)} %bitcast.6, bf16[16,2048]{1,0:T(8,128)(2,1)S(1)} %bitcast.7, bf16[1,192,128,128]{3,2,1,0:T(8,128)(2,1)S(1)} %copy-done, s32[64,192]{1,0:T(8,128)S(1)} %copy-done.4, ...), custom_call_target="tpu_custom_call" | custom-call | tf_op jit(solution)/shard_map/graph_layer/pallas_call | solution.py:403
  96.0 0.6 copy.16
  96.6 0.6 copy.17
  97.2 0.6 copy.18
  97.8 0.5 copy.19
Async XLA Ops:
  0.6 2.8 %copy-start = (bf16[1,192,128,128]{3,2,1,0:T(8,128)(2,1)S(1)}, bf16[1,192,128,128]{3,2,1,0:T(8,128)(2,1)}, u32[]{:S(2)}) copy-start(bf16[1,192,128,128]{3,2,1,0:T(8,128)(2,1)} %tv.1) | copy-start | bytes 18874372
  3.4 0.9 copy-start.1
  4.3 0.8 copy-start.2
  5.2 0.8 copy-start.3
  6.0 0.8 copy-start.4
  6.8 0.8 copy-start.5
  7.7 0.7 copy-start.6
  8.4 0.7 copy-start.7
